TPU v7x, 32 devices: a whole 2x2x4 slice. The times are simulated.
32 devices in a mesh: coil: 4 (over y, x), pencil: 8 (over z, core).
Axes of the slice: x: 2, y: 2, z: 4, core: 2. Of those that a mesh axis runs over, the one named last changes fastest.
Arguments:
- object_image: bfloat16 [32, 256, 1024], P(None, 'pencil'), may hold values from -6 to 6
- coil_maps: bfloat16 [64, 32, 256, 1024], P('coil', None, 'pencil'), may hold values from -0.75 to 0.75
- sample_mask: int32 [32, 256, 4], replicated, may hold values 0 or 1
Outputs:
- adjoint_image: float32 [32, 256, 1024], P('coil', 'pencil')
Inputs may be any that keep to these rules, and one draw needn't show every extreme that they name: `sample_mask`: 1 where the 128 readout samples of a segment are acquired.
All inputs are finite; a program needn't handle non-finite values.
Results may differ from a plain program's by a relative error of at most 0.01.
Values may be sent and summed in bfloat16 or wider, within the bound.
A program may use at most 448 MiB of HBM per device.

v0:
```python
import math

import jax
import jax.numpy as jnp
from jax import lax
from jax.sharding import PartitionSpec as P


def dft_tables(length, direction):
    indices = jnp.arange(length, dtype=jnp.int32)
    phases = indices[:, None] * indices[None, :] % length
    angles = phases.astype(jnp.float32) * (2.0 * math.pi / length)
    factor = 1.0 / math.sqrt(length)
    cosine = (jnp.cos(angles) * factor).astype(jnp.bfloat16)
    sine_part = (direction * jnp.sin(angles) * factor).astype(jnp.bfloat16)
    return (cosine, sine_part)


def readout_table(length, direction):
    cosine, sine_part = dft_tables(length, direction)
    upper = jnp.concatenate([cosine, sine_part], axis=1)
    lower = jnp.concatenate([-sine_part, cosine], axis=1)
    return jnp.concatenate([upper, lower], axis=0)


def complex_product(left_side, right_side, readout, conjugate):
    left_full = left_side.astype(jnp.float32)
    right_full = right_side.astype(jnp.float32)
    left_real = left_full[..., :readout]
    left_imag = left_full[..., readout:]
    if conjugate:
        left_imag = -left_imag
    right_real = right_full[..., :readout]
    right_imag = right_full[..., readout:]
    real_part = left_real * right_real - left_imag * right_imag
    imag_part = left_real * right_imag + left_imag * right_real
    return jnp.concatenate([real_part, imag_part], axis=-1)


def transform(volume, tables, formula, readout):
    cosine, sine_part = tables
    direct = jnp.einsum(formula, cosine, volume, preferred_element_type=jnp.float32)
    crossed = jnp.einsum(formula, sine_part, volume, preferred_element_type=jnp.float32)
    turned = jnp.concatenate([-crossed[..., readout:], crossed[..., :readout]], axis=-1)
    return (direct + turned).astype(jnp.bfloat16)


def widen(mask_part, segment):
    flags = jnp.repeat(mask_part, segment, axis=2) > 0
    return jnp.concatenate([flags, flags], axis=2)


def on_device(object_image, coil_maps, sample_mask):
    readout = object_image.shape[2] // 2
    slices = object_image.shape[0]
    row_count = object_image.shape[1]
    pencils = lax.axis_size("pencil")
    depth = slices // pencils
    lines = row_count * pencils
    segment = readout // sample_mask.shape[2]
    position = lax.axis_index("pencil")
    forward_x = readout_table(readout, -1.0)
    inverse_x = readout_table(readout, 1.0)
    forward_z = dft_tables(slices, -1.0)
    inverse_z = dft_tables(slices, 1.0)
    forward_y = dft_tables(lines, -1.0)
    inverse_y = dft_tables(lines, 1.0)
    column_mask = widen(lax.dynamic_slice_in_dim(sample_mask, position * depth, depth, 0), segment)
    nothing = jnp.zeros((), jnp.bfloat16)
    coil_image = complex_product(coil_maps, object_image[None], readout, False).astype(jnp.bfloat16)
    volume = jnp.dot(coil_image, forward_x, preferred_element_type=jnp.float32).astype(jnp.bfloat16)
    volume = transform(volume, forward_z, "kz,czyx->ckyx", readout)
    spectrum = transform(
        lax.all_to_all(volume, "pencil", split_axis=1, concat_axis=2, tiled=True),
        forward_y,
        "ky,czyx->czkx",
        readout,
    )
    spectrum = jnp.where(column_mask, spectrum, nothing)
    spectrum = transform(spectrum, inverse_y, "ky,czyx->czkx", readout)
    coil_block = lax.all_to_all(spectrum, "pencil", split_axis=2, concat_axis=1, tiled=True)
    coil_block = transform(coil_block, inverse_z, "kz,czyx->ckyx", readout)
    returned = jnp.dot(coil_block, inverse_x, preferred_element_type=jnp.float32).astype(
        jnp.bfloat16
    )
    partial_sum = jnp.sum(complex_product(coil_maps, returned, readout, True), axis=0)
    return lax.psum_scatter(
        partial_sum.astype(jnp.bfloat16), "coil", scatter_dimension=0, tiled=True
    ).astype(jnp.float32)


def solution(mesh):
    placed = (P(None, "pencil", None), P("coil", None, "pencil", None), P())
    return jax.shard_map(
        on_device, mesh=mesh, in_specs=placed, out_specs=P("coil", "pencil", None), check_vma=False
    )
```

profile of v0, /device:TPU:0, one launch (start us, length us, event | category | flops | bytes accessed | tf_op | source)
XLA Modules:
  0.0 2510.4 jit_solution(17054894281057285254)
XLA Ops:
  10.9 4.7 fusion.48
  15.6 33.2 %convert_element_type.120 = f32[16,32,32,1024]{3,2,1,0:T(8,128)} convert(bf16[16,32,32,1024]{3,2,1,0:T(8,128)(2,1)} %param.4) | non-fusion elementwise | flops 16777216 | bytes 100663296 | tf_op jit(solution)/shard_map/convert_element_type | solution.py:27
  49.9 33.7 %subtract_convert_fusion = (bf16[16,32,32,512]{3,2,1,0:T(8,128)(2,1)}, bf16[16,32,32,512]{3,2,1,0:T(8,128)(2,1)}) fusion(f32[16,32,32,1024]{3,2,1,0:T(8,128)} %convert_element_type.120, f32[32,32,512]{2,1,0:T(8,128)S(1)} %get-tuple-element.18, f32[32,32,512]{2,1,0:T(8,128)S(1)} %get-tuple-element.17), kind=kLoop, calls=%fused_computation.24 | loop fusion | flops 67108864 | bytes 104857600 | tf_op jit(solution)/shard_map/convert.1
  83.6 42.2 %fusion.18 = bf16[16,32,32,1024]{3,2,1,0:T(8,128)(2,1)} fusion(bf16[16,32,32,512]{3,2,1,0:T(8,128)(2,1)} %get-tuple-element.8, bf16[16,32,32,512]{3,2,1,0:T(8,128)(2,1)} %get-tuple-element.7, bf16[512,512]{1,0:T(8,128)(2,1)S(1)} %get-tuple-element.20, bf16[512,512]{1,0:T(8,128)(2,1)S(1)} %copy-done.5, bf16[512,512]{1,0:T(8,128)(2,1)S(1)} %get-tuple-element.19), kind=kOutput, calls=%fused_computation.33 | convolution fusion | flops 34452013056 | bytes 68681728 | tf_op jit(solution)/shard_map/dot_general | solution.py:71
  125.8 47.8 %fusion.15 = f32[16,32,32,1024]{3,1,2,0:T(8,128)} fusion(bf16[16,32,32,1024]{3,2,1,0:T(8,128)(2,1)} %fusion.18), kind=kOutput, calls=%fused_computation.29 | convolution fusion | flops 1073758208 | bytes 100663296 | tf_op jit(solution)/shard_map/kz,czyx->ckyx/dot_general | solution.py:43
  173.6 44.5 %slice_negate_fusion.3 = (f32[16,32,32,512]{3,1,2,0:T(8,128)}, f32[16,32,32,512]{3,1,2,0:T(8,128)}) fusion(f32[16,32,32,1024]{3,1,2,0:T(8,128)} %fusion.15), kind=kLoop, calls=%fused_computation.13 | loop fusion | flops 8388608 | bytes 134217728 | tf_op jit(solution)/shard_map/neg | solution.py:44
  218.0 62.4 %fusion = bf16[16,32,32,1024]{3,1,2,0:T(8,128)(2,1)} fusion(f32[16,32,32,512]{3,1,2,0:T(8,128)} %get-tuple-element.16, f32[16,32,32,512]{3,1,2,0:T(8,128)} %get-tuple-element.15, bf16[16,32,32,1024]{3,2,1,0:T(8,128)(2,1)} %fusion.18), kind=kOutput, calls=%fused_computation.1 | convolution fusion | flops 1124089856 | bytes 134217728 | tf_op jit(solution)/shard_map/kz,czyx->ckyx/dot_general | solution.py:42
  280.5 30.7 %copy.28 = bf16[16,32,32,1024]{3,2,0,1:T(8,128)(2,1)} copy(bf16[16,32,32,1024]{3,1,2,0:T(8,128)(2,1)} %fusion) | data formatting | bytes 67108864 | tf_op jit(solution)/shard_map/convert_element_type | solution.py:45
  311.2 7.3 all-to-all-start
  319.7 722.8 %all-to-all-done = bf16[16,32,32,1024]{3,2,0,1:T(8,128)(2,1)} async-done(((bf16[16,32,32,1024]{3,2,0,1:T(8,128)(2,1)}), bf16[16,32,32,1024]{3,2,0,1:T(8,128)(2,1)}, u32[]{:S(2)}, u32[]{:S(2)}) %all-to-all-start) | async-done | bytes 33554464 | tf_op jit(solution)/shard_map/all_to_all | solution.py:74
  1042.5 22.8 copy.30
  1065.3 34.3 %convolution_bitcast_fusion.2 = f32[16,4,256,1024]{2,3,1,0:T(8,128)} fusion(bf16[16,4,256,1024]{3,2,1,0:T(8,128)(2,1)} %bitcast.103), kind=kOutput, calls=%fused_computation.32 | convolution fusion | flops 8590983168 | bytes 100663296 | tf_op jit(solution)/shard_map/ky,czyx->czkx/dot_general | solution.py:43
  1099.6 42.9 %slice_negate_fusion.2 = (f32[16,4,256,512]{2,3,1,0:T(8,128)}, f32[16,4,256,512]{2,3,1,0:T(8,128)}) fusion(f32[16,4,256,1024]{2,3,1,0:T(8,128)} %convolution_bitcast_fusion.2), kind=kLoop, calls=%fused_computation.12 | loop fusion | flops 8388608 | bytes 134217728 | tf_op jit(solution)/shard_map/neg | solution.py:44
  1142.5 44.2 %fusion.4 = bf16[16,4,256,1024]{2,3,1,0:T(8,128)(2,1)} fusion(f32[16,4,256,512]{2,3,1,0:T(8,128)} %get-tuple-element.14, f32[16,4,256,512]{2,3,1,0:T(8,128)} %get-tuple-element.13, pred[4,256,1024]{1,2,0:T(8,128)(4,1)S(1)} %pad_add_fusion, bf16[16,4,256,1024]{3,2,1,0:T(8,128)(2,1)} %bitcast.104), kind=kOutput, calls=%fused_computation.9 | convolution fusion | flops 8658092032 | bytes 135266304 | tf_op jit(solution)/shard_map/ky,czyx->czkx/dot_general | solution.py:42
  1186.6 34.1 %convolution_bitcast_fusion.1 = f32[16,4,256,1024]{2,3,1,0:T(8,128)} fusion(bf16[16,4,256,1024]{2,3,1,0:T(8,128)(2,1)} %fusion.4), kind=kOutput, calls=%fused_computation.31 | convolution fusion | flops 8590983168 | bytes 100663296 | tf_op jit(solution)/shard_map/ky,czyx->czkx/dot_general | solution.py:43
  1220.8 42.9 %slice_negate_fusion.1 = (f32[16,4,256,512]{2,3,1,0:T(8,128)}, f32[16,4,256,512]{2,3,1,0:T(8,128)}) fusion(f32[16,4,256,1024]{2,3,1,0:T(8,128)} %convolution_bitcast_fusion.1), kind=kLoop, calls=%fused_computation.11 | loop fusion | flops 8388608 | bytes 134217728 | tf_op jit(solution)/shard_map/neg | solution.py:44
  1263.7 44.1 %fusion.2 = bf16[16,4,256,1024]{2,3,1,0:T(8,128)(2,1)} fusion(f32[16,4,256,512]{2,3,1,0:T(8,128)} %get-tuple-element.12, f32[16,4,256,512]{2,3,1,0:T(8,128)} %get-tuple-element.11, bf16[16,4,256,1024]{2,3,1,0:T(8,128)(2,1)} %fusion.4), kind=kOutput, calls=%fused_computation.5 | convolution fusion | flops 8641314816 | bytes 134217728 | tf_op jit(solution)/shard_map/ky,czyx->czkx/dot_general | solution.py:42
  1307.9 54.9 %copy.33 = bf16[16,4,256,1024]{3,1,0,2:T(4,128)(2,1)} copy(bf16[16,4,256,1024]{2,3,1,0:T(8,128)(2,1)} %fusion.2) | data formatting | bytes 67108864 | tf_op jit(solution)/shard_map/convert_element_type | solution.py:45
  1362.8 7.1 all-to-all-start.1
  1370.0 4.7 fusion.49
  1374.6 4.6 multiply_convert_fusion
  1379.3 713.8 %all-to-all-done.1 = bf16[16,4,256,1024]{3,1,0,2:T(4,128)(2,1)} async-done(((bf16[16,4,256,1024]{3,1,0,2:T(4,128)(2,1)}), bf16[16,4,256,1024]{3,1,0,2:T(4,128)(2,1)}, u32[]{:S(2)}, u32[]{:S(2)}) %all-to-all-start.1) | async-done | bytes 33554464 | tf_op jit(solution)/shard_map/all_to_all | solution.py:81
  2093.1 23.5 copy.34
  2116.6 42.2 %copy.35 = bf16[16,8,4,32,1024]{4,2,1,3,0:T(4,128)(2,1)} copy(bf16[16,8,4,32,1024]{4,3,1,2,0:T(8,128)(2,1)} %bitcast.105) | data formatting | bytes 67108864 | tf_op jit(solution)/shard_map/all_to_all | solution.py:81
  2158.8 45.9 %all_to_all.33 = bf16[16,32,32,1024]{3,1,2,0:T(8,128)(2,1)} reshape(bf16[16,8,4,32,1024]{4,2,1,3,0:T(4,128)(2,1)} %copy.35) | data formatting | bytes 67108864 | tf_op jit(solution)/shard_map/all_to_all | solution.py:81
  2204.7 33.4 %convolution_bitcast_fusion = f32[16,32,32,1024]{3,1,2,0:T(8,128)} fusion(bf16[16,32,32,1024]{3,1,2,0:T(8,128)(2,1)} %all_to_all.33), kind=kOutput, calls=%fused_computation.30 | convolution fusion | flops 1073758208 | bytes 100663296 | tf_op jit(solution)/shard_map/kz,czyx->ckyx/dot_general | solution.py:43
  2238.1 44.5 %slice_negate_fusion = (f32[16,32,32,512]{3,1,2,0:T(8,128)}, f32[16,32,32,512]{3,1,2,0:T(8,128)}) fusion(f32[16,32,32,1024]{3,1,2,0:T(8,128)} %convolution_bitcast_fusion), kind=kLoop, calls=%fused_computation.10 | loop fusion | flops 8388608 | bytes 134217728 | tf_op jit(solution)/shard_map/neg | solution.py:44
  2282.5 42.9 %fusion.3 = bf16[16,32,32,1024]{3,1,2,0:T(8,128)(2,1)} fusion(f32[16,32,32,512]{3,1,2,0:T(8,128)} %get-tuple-element.10, f32[16,32,32,512]{3,1,2,0:T(8,128)} %get-tuple-element.9, bf16[16,32,32,1024]{3,1,2,0:T(8,128)(2,1)} %all_to_all.33), kind=kOutput, calls=%fused_computation.7 | convolution fusion | flops 1124089856 | bytes 134217728 | tf_op jit(solution)/shard_map/kz,czyx->ckyx/dot_general | solution.py:42
  2325.4 53.6 %convert_convert_fusion = f32[16,32,32,1024]{3,2,1,0:T(8,128)} fusion(bf16[16,32,32,1024]{3,1,2,0:T(8,128)(2,1)} %fusion.3, bf16[512,512]{1,0:T(8,128)(2,1)S(1)} %copy-done.2, bf16[512,512]{1,0:T(8,128)(2,1)S(1)} %copy-done.3, bf16[512,512]{1,0:T(8,128)(2,1)S(1)} %copy-done.4), kind=kOutput, calls=%fused_computation.22 | convolution fusion | flops 34401681408 | bytes 102236160 | tf_op jit(solution)/shard_map/dot_general | solution.py:83
  2379.0 64.5 %multiply_subtract_fusion = (f32[16,32,32,512]{3,2,1,0:T(8,128)}, f32[16,32,32,512]{3,2,1,0:T(8,128)}) fusion(f32[16,32,32,1024]{3,2,1,0:T(8,128)} %convert_convert_fusion, f32[16,32,32,1024]{3,2,1,0:T(8,128)} %convert_element_type.120), kind=kLoop, calls=%fused_computation.21 | loop fusion | flops 58720256 | bytes 201326592 | tf_op jit(solution)/shard_map/sub | solution.py:35
  2443.5 22.5 maximum_reduce_fusion
  2466.1 34.9 %reduce-scatter.2.cloned.1.call-done = bf16[8,32,1024]{2,1,0:T(8,128)(2,1)} async-done(((bf16[32,32,1024]{2,1,0:T(8,128)(2,1)}), bf16[8,32,1024]{2,1,0:T(8,128)(2,1)}) %reduce-scatter.2.cloned.1.call-update) | async-done | bytes 524304 | tf_op jit(solution)/shard_map/reduce_scatter | solution.py:87
  (21 shorter events, 8.9 us)
Async XLA Ops:
  10.9 72.7 %copy-start.1 = (bf16[512,512]{1,0:T(8,128)(2,1)}, bf16[512,512]{1,0:T(8,128)(2,1)S(1)}, u32[]{:S(2)}) copy-start(bf16[512,512]{1,0:T(8,128)(2,1)S(1)} %get-tuple-element.20) | copy-start | bytes 1572868
  15.6 33.2 %copy-start = (bf16[32,32,1024]{2,1,0:T(8,128)(2,1)S(1)}, bf16[32,32,1024]{2,1,0:T(8,128)(2,1)}, u32[]{:S(2)}) copy-start(bf16[32,32,1024]{2,1,0:T(8,128)(2,1)} %param.3) | copy-start | bytes 6291460
  49.9 33.7 %copy-start.5 = (bf16[512,512]{1,0:T(8,128)(2,1)S(1)}, bf16[512,512]{1,0:T(8,128)(2,1)}, u32[]{:S(2)}) copy-start(bf16[512,512]{1,0:T(8,128)(2,1)} %fusion.48) | copy-start | bytes 1572868
  311.2 731.3 %all-to-all-start = ((bf16[16,32,32,1024]{3,2,0,1:T(8,128)(2,1)}), bf16[16,32,32,1024]{3,2,0,1:T(8,128)(2,1)}, u32[]{:S(2)}, u32[]{:S(2)}) async-start(bf16[16,32,32,1024]{3,2,0,1:T(8,128)(2,1)} %copy.28), calls=%async_computation | async-start | bytes 67108864 | tf_op jit(solution)/shard_map/all_to_all | solution.py:74
  1362.8 730.3 %all-to-all-start.1 = ((bf16[16,4,256,1024]{3,1,0,2:T(4,128)(2,1)}), bf16[16,4,256,1024]{3,1,0,2:T(4,128)(2,1)}, u32[]{:S(2)}, u32[]{:S(2)}) async-start(bf16[16,4,256,1024]{3,1,0,2:T(4,128)(2,1)} %copy.33), calls=%async_computation.1 | async-start | bytes 67108864 | tf_op jit(solution)/shard_map/all_to_all | solution.py:81
  1369.9 1131.1 %reduce-scatter.2.cloned.1.call-start = ((), (), s32[]{:S(2)}) async-start(), calls=%async_computation.3 | async-start | bytes 2621440 | tf_op jit(solution)/shard_map/reduce_scatter | solution.py:87
  2282.5 42.9 %copy-start.2 = (bf16[512,512]{1,0:T(8,128)(2,1)S(1)}, bf16[512,512]{1,0:T(8,128)(2,1)}, u32[]{:S(2)}) copy-start(bf16[512,512]{1,0:T(8,128)(2,1)} %copy-done.1) | copy-start | bytes 1572868
  2282.5 42.9 %copy-start.3 = (bf16[512,512]{1,0:T(8,128)(2,1)S(1)}, bf16[512,512]{1,0:T(8,128)(2,1)}, u32[]{:S(2)}) copy-start(bf16[512,512]{1,0:T(8,128)(2,1)} %fusion.49) | copy-start | bytes 1572868
  2282.5 42.9 %copy-start.4 = (bf16[512,512]{1,0:T(8,128)(2,1)S(1)}, bf16[512,512]{1,0:T(8,128)(2,1)}, u32[]{:S(2)}) copy-start(bf16[512,512]{1,0:T(8,128)(2,1)} %multiply_convert_fusion) | copy-start | bytes 1572868
Sparse Core Ops, SparseCore 0:
  2466.2 34.7 reduce-scatter.1
where the time goes:
time: 2520 us; the launch traced here: 2510 us
  waiting for transfers between devices  1470 us (58%)
  matrix products  439 us (17%)
  other arithmetic  351 us (14%)
  local copies, waits for them, and re-layouts  221 us (9%)
    all_to_all x1, waiting for transfers between devices, on_device(): lax.all_to_all(volume, 'pencil', split_axis=1, concat_axis=2, tiled=True)  723 us
    all_to_all x1, waiting for transfers between devices, on_device(): lax.all_to_all(spectrum, 'pencil', split_axis=2, concat_axis=1, tiled=True)  714 us
    dot_general x4, matrix products, transform(): jnp.einsum(formula, cosine, volume, preferred_element_type=jnp.float32)  194 us
    neg x4, other arithmetic, transform(): -crossed[..., readout:]  175 us
    dot_general x4, matrix products, transform(): jnp.einsum(formula, sine_part, volume, preferred_element_type=jnp.float32)  150 us
    all_to_all x3, local copies, waits for them, and re-layouts, on_device(): lax.all_to_all(spectrum, 'pencil', split_axis=2, concat_axis=1, tiled=True)  112 us
    convert_element_type x2, local copies, waits for them, and re-layouts, transform(): return (direct + turned).astype(jnp.bfloat16)  85.6 us
    sub x1, other arithmetic, complex_product(): real_part = left_real * right_real - left_imag * right_imag  64.5 us
  transfers between devices with their start and end apart: 3, of which 3 were waited for; matrix products, arithmetic and copies ran while one was open for 0% of the time, Pallas kernels for 0%

commit v1 on v0

--- a/solution.py
+++ b/solution.py
@@ -3,6 +3,8 @@
 import jax
 import jax.numpy as jnp
 from jax import lax
+from jax.experimental import pallas as pl
+from jax.experimental.pallas import tpu as pltpu
 from jax.sharding import PartitionSpec as P
 
 
@@ -50,7 +52,7 @@
     return jnp.concatenate([flags, flags], axis=2)
 
 
-def on_device(object_image, coil_maps, sample_mask):
+def split_lines(object_image, coil_maps, sample_mask):
     readout = object_image.shape[2] // 2
     slices = object_image.shape[0]
     row_count = object_image.shape[1]
@@ -89,8 +91,386 @@
     ).astype(jnp.float32)
 
 
+MESH = pl.DeviceIdType.MESH
+
+
+def rotation(cosine, sine_part, rows):
+    if rows:
+        upper = jnp.concatenate([cosine, sine_part], axis=1)
+        lower = jnp.concatenate([-sine_part, cosine], axis=1)
+    else:
+        upper = jnp.concatenate([cosine, -sine_part], axis=1)
+        lower = jnp.concatenate([sine_part, cosine], axis=1)
+    return jnp.concatenate([upper, lower], axis=0)
+
+
+def plan_tables(slices, lines, readout, group):
+    eye = jnp.eye(group, dtype=jnp.bfloat16)
+    quarter, half_y, half_z = readout // 4, lines // 2, slices // 2
+    cx, sx = dft_tables(readout, -1.0)
+    x_fwd = jnp.stack([rotation(cx[:quarter, r::4], sx[:quarter, r::4], True) for r in range(4)])
+    cx, sx = dft_tables(readout, 1.0)
+    x_inv = jnp.stack([rotation(cx[r::4, :quarter], sx[r::4, :quarter], True) for r in range(4)])
+    cy, sy = dft_tables(lines, -1.0)
+    y_fwd = jnp.stack([rotation(cy[p::2, :half_y], sy[p::2, :half_y], False) for p in range(2)])
+    cy, sy = dft_tables(lines, 1.0)
+    y_inv = jnp.stack([rotation(cy[:half_y, p::2], sy[:half_y, p::2], False) for p in range(2)])
+    cz, sz = dft_tables(slices, -1.0)
+    z_fwd = jnp.stack(
+        [
+            rotation(jnp.kron(cz[p::2, :half_z], eye), jnp.kron(sz[p::2, :half_z], eye), False)
+            for p in range(2)
+        ]
+    )
+    cz, sz = dft_tables(slices, 1.0)
+    z_inv = jnp.stack(
+        [
+            rotation(jnp.kron(cz[:half_z, p::2], eye), jnp.kron(sz[:half_z, p::2], eye), False)
+            for p in range(2)
+        ]
+    )
+    return x_fwd, x_inv, y_fwd, y_inv, z_fwd, z_inv
+
+
+def mm(left, right):
+    return jnp.dot(left, right, preferred_element_type=jnp.float32)
+
+
+def forward_body(map_part, image_part, x_fwd, y_fwd):
+    lines = map_part.shape[0]
+    readout = map_part.shape[1] // 2
+    quarter, half = readout // 4, lines // 2
+    left = map_part.astype(jnp.float32)
+    right = image_part.astype(jnp.float32)
+    re, im = [], []
+    for q in range(4):
+        a, b = q * quarter, (q + 1) * quarter
+        lr, li = left[:, a:b], left[:, readout + a : readout + b]
+        rr, ri = right[:, a:b], right[:, readout + a : readout + b]
+        re.append(lr * rr - li * ri)
+        im.append(lr * ri + li * rr)
+    sum_re, sum_im = re[0] + re[2], im[0] + im[2]
+    dif_re, dif_im = re[0] - re[2], im[0] - im[2]
+    odd_re, odd_im = re[1] + re[3], im[1] + im[3]
+    tur_re, tur_im = re[1] - re[3], im[1] - im[3]
+    mixed = [
+        (sum_re + odd_re, sum_im + odd_im),
+        (dif_re + tur_im, dif_im - tur_re),
+        (sum_re - odd_re, sum_im - odd_im),
+        (dif_re - tur_im, dif_im + tur_re),
+    ]
+    even, odd = [], []
+    for r in range(4):
+        v = mm(jnp.concatenate(mixed[r], axis=1).astype(jnp.bfloat16), x_fwd[r])
+        e = (v[:half] + v[half:]).astype(jnp.bfloat16)
+        o = (v[:half] - v[half:]).astype(jnp.bfloat16)
+        even.append(jnp.concatenate([e[:, :quarter], e[:, quarter:]], axis=0))
+        odd.append(jnp.concatenate([o[:, :quarter], o[:, quarter:]], axis=0))
+    even = mm(y_fwd[0], jnp.concatenate(even, axis=1)).astype(jnp.bfloat16)
+    odd = mm(y_fwd[1], jnp.concatenate(odd, axis=1)).astype(jnp.bfloat16)
+    return even, odd
+
+
+def slab_body(block, mask_block, z_fwd, z_inv):
+    slices, group, width = block.shape
+    half, readout = slices // 2, width // 2
+    flat = half * group
+    low = block[:half].astype(jnp.float32)
+    high = block[half:].astype(jnp.float32)
+    parts = [low + high, low - high]
+    back = []
+    for p in range(2):
+        u = parts[p].astype(jnp.bfloat16).reshape(flat, width)
+        u = jnp.concatenate([u[:, :readout], u[:, readout:]], axis=0)
+        k = mm(z_fwd[p], u)
+        m = mask_block[p].reshape(flat, readout).astype(jnp.float32)
+        k = jnp.concatenate([k[:flat] * m, k[flat:] * m], axis=0).astype(jnp.bfloat16)
+        back.append(mm(z_inv[p], k))
+
+    def place(t):
+        t = t.astype(jnp.bfloat16)
+        return jnp.concatenate([t[:flat], t[flat:]], axis=1).reshape(half, group, width)
+
+    return place(back[0] + back[1]), place(back[0] - back[1])
+
+
+def backward_body(block, map_part, x_inv, y_inv):
+    lines = block.shape[0]
+    readout = block.shape[1] // 2
+    quarter, half = readout // 4, lines // 2
+    sides = []
+    for p in range(2):
+        part = block[p * half : (p + 1) * half]
+        sides.append(mm(y_inv[p], jnp.concatenate([part[:, :readout], part[:, readout:]], axis=0)))
+    lows = (sides[0] + sides[1]).astype(jnp.bfloat16)
+    highs = (sides[0] - sides[1]).astype(jnp.bfloat16)
+    t_re, t_im = [], []
+    for r in range(4):
+        a, b = r * quarter, (r + 1) * quarter
+        rows = jnp.concatenate(
+            [
+                jnp.concatenate([lows[:half, a:b], lows[half:, a:b]], axis=1),
+                jnp.concatenate([highs[:half, a:b], highs[half:, a:b]], axis=1),
+            ],
+            axis=0,
+        )
+        t = mm(rows, x_inv[r])
+        t_re.append(t[:, :quarter])
+        t_im.append(t[:, quarter:])
+    sr, si = t_re[0] + t_re[2], t_im[0] + t_im[2]
+    dr, di = t_re[0] - t_re[2], t_im[0] - t_im[2]
+    er, ei = t_re[1] + t_re[3], t_im[1] + t_im[3]
+    fr, fi = t_re[1] - t_re[3], t_im[1] - t_im[3]
+    image = [(sr + er, si + ei), (dr - fi, di + fr), (sr - er, si - ei), (dr + fi, di - fr)]
+    maps = map_part.astype(jnp.float32)
+    out_re, out_im = [], []
+    for q in range(4):
+        a, b = q * quarter, (q + 1) * quarter
+        mr, mi = maps[:, a:b], maps[:, readout + a : readout + b]
+        xr, xi = image[q]
+        out_re.append(mr * xr + mi * xi)
+        out_im.append(mr * xi - mi * xr)
+    return jnp.concatenate(out_re + out_im, axis=1)
+
+
+def image_rows(image_ref):
+    chips = image_ref.shape[2]
+    return jnp.concatenate([image_ref[i % 2, 0, i // 2] for i in range(2 * chips)], axis=0)
+
+
+def forward_call(maps, image, x_fwd, y_fwd):
+    coils, slices, lines, width = maps.shape
+    chips, rows = image.shape[2], image.shape[3]
+    half = lines // 2
+
+    def body(map_ref, image_ref, x_ref, y_ref, out_ref):
+        even, odd = forward_body(map_ref[0, 0], image_rows(image_ref), x_ref[...], y_ref[...])
+        readout = even.shape[1]
+        out_ref[0, 0, :half, :readout] = even[:half]
+        out_ref[0, 0, :half, readout:] = even[half:]
+        out_ref[0, 0, half:, :readout] = odd[:half]
+        out_ref[0, 0, half:, readout:] = odd[half:]
+
+    return pl.pallas_call(
+        body,
+        grid=(slices, coils),
+        out_shape=jax.ShapeDtypeStruct(maps.shape, jnp.bfloat16),
+        in_specs=[
+            pl.BlockSpec((1, 1, lines, width), lambda z, j: (j, z, 0, 0)),
+            pl.BlockSpec((2, 1, chips, rows, width), lambda z, j: (0, z, 0, 0, 0)),
+            pl.BlockSpec(x_fwd.shape, lambda z, j: (0, 0, 0)),
+            pl.BlockSpec(y_fwd.shape, lambda z, j: (0, 0, 0)),
+        ],
+        out_specs=pl.BlockSpec((1, 1, lines, width), lambda z, j: (j, z, 0, 0)),
+        compiler_params=pltpu.CompilerParams(vmem_limit_bytes=48 << 20),
+        name="forward_xy",
+    )(maps, image, x_fwd, y_fwd)
+
+
+def slab_call(volume, mask, z_fwd, z_inv, group):
+    coils, slices, lines, width = volume.shape
+    half = slices // 2
+
+    def body(block_ref, mask_ref, f_ref, b_ref, out_ref):
+        low, high = slab_body(block_ref[0], mask_ref[...], f_ref[...], b_ref[...])
+        out_ref[0, :half] = low
+        out_ref[0, half:] = high
+
+    return pl.pallas_call(
+        body,
+        grid=(lines // group, coils),
+        out_shape=jax.ShapeDtypeStruct(volume.shape, jnp.bfloat16),
+        in_specs=[
+            pl.BlockSpec((1, slices, group, width), lambda y, j: (j, 0, y, 0)),
+            pl.BlockSpec((2, half, group, width // 2), lambda y, j: (0, 0, y, 0)),
+            pl.BlockSpec(z_fwd.shape, lambda y, j: (0, 0, 0)),
+            pl.BlockSpec(z_inv.shape, lambda y, j: (0, 0, 0)),
+        ],
+        out_specs=pl.BlockSpec((1, slices, group, width), lambda y, j: (j, 0, y, 0)),
+        compiler_params=pltpu.CompilerParams(vmem_limit_bytes=48 << 20),
+        name="slab_mask",
+    )(volume, mask, z_fwd, z_inv)
+
+
+def backward_call(volume, maps, x_inv, y_inv):
+    coils, slices, lines, width = volume.shape
+
+    def body(block_ref, map_ref, x_ref, y_ref, out_ref):
+        total = backward_body(block_ref[0, 0], map_ref[0, 0], x_ref[...], y_ref[...])
+        for j in range(1, coils):
+            total += backward_body(block_ref[j, 0], map_ref[j, 0], x_ref[...], y_ref[...])
+        out_ref[0] = total.astype(out_ref.dtype)
+
+    return pl.pallas_call(
+        body,
+        grid=(slices,),
+        out_shape=jax.ShapeDtypeStruct((slices, lines, width), jnp.bfloat16),
+        in_specs=[
+            pl.BlockSpec((coils, 1, lines, width), lambda z: (0, z, 0, 0)),
+            pl.BlockSpec((coils, 1, lines, width), lambda z: (0, z, 0, 0)),
+            pl.BlockSpec(x_inv.shape, lambda z: (0, 0, 0)),
+            pl.BlockSpec(y_inv.shape, lambda z: (0, 0, 0)),
+        ],
+        out_specs=pl.BlockSpec((1, lines, width), lambda z: (z, 0, 0)),
+        compiler_params=pltpu.CompilerParams(vmem_limit_bytes=56 << 20),
+        name="backward_yx",
+    )(volume, maps, x_inv, y_inv)
+
+
+def exchange_call(coil_maps, object_image):
+    pencils, columns = lax.axis_size("pencil"), lax.axis_size("coil")
+    coils, slices, rows, width = coil_maps.shape
+    per, chips, share = coils // pencils, pencils // 2, slices // columns
+    shifts = sorted(range(1, pencils), key=lambda s: abs(s - pencils // 2))
+
+    def kernel(
+        map_ref, image_ref, out_ref, full_ref, own_sem, map_send, map_recv, im_send, im_recv,
+        col_send, col_recv, core_send, core_recv,
+    ):
+        me, column = lax.axis_index("pencil"), lax.axis_index("coil")
+        chip, core = me // 2, me % 2
+
+        barrier = pltpu.get_barrier_semaphore()
+        for s in range(1, pencils):
+            pl.semaphore_signal(
+                barrier, device_id=(column, lax.rem(me + s, pencils)), device_id_type=MESH
+            )
+        for s in range(1, columns):
+            pl.semaphore_signal(
+                barrier, device_id=(lax.rem(column + s, columns), me), device_id_type=MESH
+            )
+        pl.semaphore_wait(barrier, pencils + columns - 2)
+
+        quarter = pl.ds(column * share, share)
+        own = [
+            pltpu.make_async_copy(
+                image_ref.at[quarter], full_ref.at[core, quarter, chip], own_sem.at[per]
+            )
+        ]
+        for j in range(per):
+            own.append(
+                pltpu.make_async_copy(
+                    map_ref.at[me * per + j], out_ref.at[j, :, pl.ds(me * rows, rows)], own_sem.at[j]
+                )
+            )
+        along = []
+        for i, s in enumerate(range(1, chips)):
+            along.append(
+                pltpu.make_async_remote_copy(
+                    src_ref=image_ref.at[quarter],
+                    dst_ref=full_ref.at[core, quarter, chip],
+                    send_sem=im_send.at[i],
+                    recv_sem=im_recv.at[i],
+                    device_id=(column, lax.rem(me + 2 * s, pencils)),
+                    device_id_type=MESH,
+                )
+            )
+        moves = []
+        for j in range(per):
+            for i, s in enumerate(shifts):
+                target = lax.rem(me + s, pencils)
+                moves.append(
+                    pltpu.make_async_remote_copy(
+                        src_ref=map_ref.at[target * per + j],
+                        dst_ref=out_ref.at[j, :, pl.ds(me * rows, rows)],
+                        send_sem=map_send.at[j, i],
+                        recv_sem=map_recv.at[j, i],
+                        device_id=(column, target),
+                        device_id_type=MESH,
+                    )
+                )
+        for copy in along + moves + own:
+            copy.start()
+        own[0].wait()
+        for copy in along:
+            copy.wait()
+        across = []
+        for i, s in enumerate(range(1, columns)):
+            across.append(
+                pltpu.make_async_remote_copy(
+                    src_ref=full_ref.at[core, quarter],
+                    dst_ref=full_ref.at[core, quarter],
+                    send_sem=col_send.at[i],
+                    recv_sem=col_recv.at[i],
+                    device_id=(lax.rem(column + s, columns), me),
+                    device_id_type=MESH,
+                )
+            )
+        for copy in across:
+            copy.start()
+        for copy in across:
+            copy.wait()
+        pair = pltpu.make_async_remote_copy(
+            src_ref=full_ref.at[core],
+            dst_ref=full_ref.at[core],
+            send_sem=core_send,
+            recv_sem=core_recv,
+            device_id=(column, me + 1 - 2 * core),
+            device_id_type=MESH,
+        )
+        pair.start()
+        pair.wait()
+        for copy in own[1:] + moves:
+            copy.wait()
+
+    dma = pltpu.SemaphoreType.DMA
+    anywhere = pl.BlockSpec(memory_space=pl.ANY)
+    return pl.pallas_call(
+        kernel,
+        out_shape=[
+            jax.ShapeDtypeStruct((per, slices, rows * pencils, width), jnp.bfloat16),
+            jax.ShapeDtypeStruct((2, slices, chips, rows, width), jnp.bfloat16),
+        ],
+        in_specs=[anywhere, anywhere],
+        out_specs=[anywhere, anywhere],
+        scratch_shapes=[
+            dma((per + 1,)),
+            dma((per, pencils - 1)),
+            dma((per, pencils - 1)),
+            dma((chips - 1,)),
+            dma((chips - 1,)),
+            dma((columns - 1,)),
+            dma((columns - 1,)),
+            dma,
+            dma,
+        ],
+        compiler_params=pltpu.CompilerParams(collective_id=0, has_side_effects=True),
+        name="exchange_maps",
+    )(coil_maps, object_image)
+
+
+def plan_mask(sample_mask, readout):
+    slices, lines, segments = sample_mask.shape
+    run = readout // segments // 4
+    flags = sample_mask.reshape(slices // 2, 2, lines // 2, 2, segments).transpose(1, 0, 3, 2, 4)
+    flags = (flags > 0).astype(jnp.bfloat16).reshape(2, slices // 2, lines, segments)
+    return jnp.tile(jnp.repeat(flags, run, axis=3), (1, 1, 1, 4))
+
+
+def whole_coils(object_image, coil_maps, sample_mask):
+    readout = object_image.shape[2] // 2
+    slices = object_image.shape[0]
+    lines = object_image.shape[1] * lax.axis_size("pencil")
+    group = 16
+    x_fwd, x_inv, y_fwd, y_inv, z_fwd, z_inv = plan_tables(slices, lines, readout, group)
+    mask = plan_mask(sample_mask, readout)
+    maps, image = exchange_call(coil_maps, object_image)
+    volume = forward_call(maps, image, x_fwd, y_fwd)
+    volume = slab_call(volume, mask, z_fwd, z_inv, group)
+    partial_sum = backward_call(volume, maps, x_inv, y_inv)
+    partial_sum = lax.psum_scatter(partial_sum, "coil", scatter_dimension=0, tiled=True)
+    return lax.psum_scatter(partial_sum, "pencil", scatter_dimension=1, tiled=True).astype(
+        jnp.float32
+    )
+
+
 def solution(mesh):
     placed = (P(None, "pencil", None), P("coil", None, "pencil", None), P())
+
+    def on_device(object_image, coil_maps, sample_mask):
+        whole = coil_maps.shape[0] % lax.axis_size("pencil") == 0
+        return (whole_coils if whole else split_lines)(object_image, coil_maps, sample_mask)
+
     return jax.shard_map(
         on_device, mesh=mesh, in_specs=placed, out_specs=P("coil", "pencil", None), check_vma=False
     )

time: 2520 us -> 1280 us (0.51)
  waiting for transfers between devices: 1470 us -> 296 us
  Pallas kernels: 0 us -> 857 us
  matrix products: 439 us -> 0 us
  other arithmetic: 351 us -> 37.9 us
  local copies, waits for them, and re-layouts: 221 us -> 70.4 us
    all_to_all x2 -> x0, waiting for transfers between devices: 1440 us -> none  [the longest x1 723 us: on_device(): lax.all_to_all(volume, 'pencil', split_axis=1, concat_axis=2, tiled=True)]
    pallas_call x0 -> x4, Pallas kernels: none -> 857 us  [the longest x1 681 us: exchange_call(): pl.pallas_call(kernel, out_shape=[jax.ShapeDtypeStruct((per, slices, rows...]
    dot_general x10 -> x0, matrix products: 439 us -> none  [the longest x4 194 us: transform(): jnp.einsum(formula, cosine, volume, preferred_element_type=jnp.float32)]
    reduce_scatter x1 -> x2, waiting for transfers between devices: 34.9 us -> 296 us  [the longest x1 244 us: whole_coils(): lax.psum_scatter(partial_sum, 'coil', scatter_dimension=0, tiled=True)]
    neg x6 -> x16, other arithmetic: 184 us -> 14 us  [the longest x8 7.92 us: rotation(): lower = jnp.concatenate([-sine_part, cosine], axis=1)]
    all_to_all x4 -> x0, local copies, waits for them, and re-layouts: 134 us -> none  [the longest x3 112 us: on_device(): lax.all_to_all(spectrum, 'pencil', split_axis=2, concat_axis=1, tiled=True)]
    convert_element_type x2 -> x0, local copies, waits for them, and re-layouts: 85.6 us -> none  [transform(): return (direct + turned).astype(jnp.bfloat16)]
    sub x1 -> x0, other arithmetic: 64.5 us -> none  [complex_product(): real_part = left_real * right_real - left_imag * right_imag]
  transfers between devices with their start and end apart: 3 -> 2, of which waited for: 3 -> 2; matrix products, arithmetic and copies ran while one was open for 0% -> 0% of each run, Pallas kernels for 0% -> 0%
where the time goes in v1:
time: 1280 us
  Pallas kernels  857 us (67%)
  waiting for transfers between devices  296 us (23%)
  local copies, waits for them, and re-layouts  70.4 us (6%)
  other arithmetic  37.9 us (3%)
  between operations  14.2 us (1%)
    pallas_call x1, Pallas kernels, exchange_call(): pl.pallas_call(kernel, out_shape=[jax.ShapeDtypeStruct((per, slices, rows...  681 us
    reduce_scatter x1, waiting for transfers between devices, whole_coils(): lax.psum_scatter(partial_sum, 'coil', scatter_dimension=0, tiled=True)  244 us
    pallas_call x1, Pallas kernels, forward_call(): pl.pallas_call(body, grid=(slices, coils), out_shape=jax.ShapeDtypeStruct...  71.3 us
    pallas_call x1, Pallas kernels, slab_call(): pl.pallas_call(body, grid=(lines // group, coils), out_shape=jax.ShapeDty...  53.6 us
    reduce_scatter x1, waiting for transfers between devices, whole_coils(): lax.psum_scatter(partial_sum, 'pencil', scatter_dimension=1, tiled=True)  52.3 us
    pallas_call x1, Pallas kernels, backward_call(): pl.pallas_call(body, grid=(slices,), out_shape=jax.ShapeDtypeStruct((slic...  51.3 us
  transfers between devices with their start and end apart: 2, of which 2 were waited for; matrix products, arithmetic and copies ran while one was open for 0% of the time, Pallas kernels for 0%

profile of v1, /device:TPU:0, one launch (start us, length us, event | category | flops | bytes accessed | tf_op | source)
XLA Modules:
  0.0 1275.5 jit_solution(6645329482773020971)
XLA Ops:
  7.4 4.0 multiply_convert_fusion.2
  11.3 1.8 slice.160
  13.1 1.8 slice.162
  14.9 4.0 multiply_convert_fusion.1
  18.9 1.8 slice.161
  20.6 1.8 slice.163
  22.4 1.8 slice.164
  24.1 1.7 slice.166
  25.9 1.8 slice.165
  27.6 1.7 slice.167
  35.2 4.0 multiply_convert_fusion
  43.1 1.8 slice.188
  44.9 1.7 slice.190
  47.6 1.8 slice.189
  49.4 1.7 slice.191
  51.1 2.6 broadcast_multiply_fusion.2
  53.7 2.2 mul.946
  56.6 2.2 mul.952
  59.5 2.8 mul.941
  62.4 2.8 mul.949
  65.2 2.2 mul.959
  82.7 1.5 broadcast_in_dim.33
  84.2 3.0 copy.7
  87.3 5.5 tile.11
  92.8 13.2 %tile.12.mask_ref = bf16[2,16,256,512]{3,2,1,0:T(8,128)(2,1)} reshape(bf16[2,16,256,4,128]{4,3,2,1,0:T(4,128)(2,1)} %tile.11) | data formatting | bytes 16777216 | tf_op jit(solution)/shard_map/tile | solution.py:447
  111.3 681.0 %exchange_maps.1 = (bf16[2,32,256,1024]{3,2,1,0:T(8,128)(2,1)}, bf16[2,32,4,32,1024]{4,3,2,1,0:T(8,128)(2,1)}) custom-call(bf16[16,32,32,1024]{3,2,1,0:T(8,128)(2,1)} %map_ref.1, bf16[32,32,1024]{2,1,0:T(8,128)(2,1)} %image_ref.1), custom_call_target="tpu_custom_call" | custom-call | tf_op jit(solution)/shard_map/exchange_maps/pallas_call | solution.py:418
  793.3 71.3 %forward_xy.1.block_ref = bf16[2,32,256,1024]{3,2,1,0:T(8,128)(2,1)} custom-call(bf16[2,32,256,1024]{3,2,1,0:T(8,128)(2,1)} %get-tuple-element.7.map_ref, bf16[2,32,4,32,1024]{4,3,2,1,0:T(8,128)(2,1)} %get-tuple-element.8.image_ref, bf16[4,256,256]{2,1,0:T(8,128)(2,1)S(1)} %pad_maximum_fusion.2.x_ref, bf16[2,256,256]{2,1,0:T(8,128)(2,1)S(1)} %pad_maximum_fusion.4.y_ref), custom_call_target="tpu_custom_call" | custom-call | tf_op jit(solution)/shard_map/forward_xy/pallas_call | solution.py:254
  864.7 53.6 %slab_mask.1.block_ref = bf16[2,32,256,1024]{3,2,1,0:T(8,128)(2,1)} custom-call(bf16[2,32,256,1024]{3,2,1,0:T(8,128)(2,1)} %forward_xy.1.block_ref, bf16[2,16,256,512]{3,2,1,0:T(8,128)(2,1)} %tile.12.mask_ref, bf16[2,512,512]{2,1,0:T(8,128)(2,1)S(1)} %pad_maximum_fusion.f_ref, bf16[2,512,512]{2,1,0:T(8,128)(2,1)S(1)} %pad_maximum_fusion.1.b_ref), custom_call_target="tpu_custom_call" | custom-call | tf_op jit(solution)/shard_map/slab_mask/pallas_call | solution.py:279
  919.3 51.3 %backward_yx.1 = bf16[32,256,1024]{2,1,0:T(8,128)(2,1)} custom-call(bf16[2,32,256,1024]{3,2,1,0:T(8,128)(2,1)} %slab_mask.1.block_ref, bf16[2,32,256,1024]{3,2,1,0:T(8,128)(2,1)} %get-tuple-element.7.map_ref, bf16[4,256,256]{2,1,0:T(8,128)(2,1)} %pad_maximum_fusion.3.x_ref, bf16[2,256,256]{2,1,0:T(8,128)(2,1)} %pad_maximum_fusion.5.y_ref), custom_call_target="tpu_custom_call" | custom-call | tf_op jit(solution)/shard_map/backward_yx/pallas_call | solution.py:304
  970.7 243.5 %reduce-scatter.3.cloned.1.call-done = bf16[8,256,1024]{2,1,0:T(8,128)(2,1)} async-done(((bf16[32,256,1024]{2,1,0:T(8,128)(2,1)}), bf16[8,256,1024]{2,1,0:T(8,128)(2,1)}) %reduce-scatter.3.cloned.1.call-update) | async-done | bytes 4194320 | tf_op jit(solution)/shard_map/reduce_scatter | solution.py:461
  1214.2 52.3 %reduce-scatter.5.cloned.1.call-done = bf16[8,32,1024]{2,1,0:T(8,128)(2,1)} async-done(((bf16[8,256,1024]{2,1,0:T(8,128)(2,1)}), bf16[8,32,1024]{2,1,0:T(8,128)(2,1)}) %reduce-scatter.5.cloned.1.call-update) | async-done | bytes 524304 | tf_op jit(solution)/shard_map/reduce_scatter | solution.py:462
  1266.5 2.1 convert_element_type.336
  (154 shorter events, 35.2 us)
Async XLA Ops:
  6.5 1207.7 %reduce-scatter.3.cloned.1.call-start = ((), (), s32[]{:S(2)}) async-start(), calls=%async_computation.2 | async-start | bytes 20971520 | tf_op jit(solution)/shard_map/reduce_scatter | solution.py:461
  111.1 681.2 %copy-start.20 = (bf16[128,128]{1,0:T(8,128)(2,1)S(1)}, bf16[128,128]{1,0:T(8,128)(2,1)}, u32[]{:S(2)}) copy-start(bf16[128,128]{1,0:T(8,128)(2,1)} %slice.189) | copy-start | bytes 98308
  111.1 681.2 %copy-start.22 = (bf16[128,128]{1,0:T(8,128)(2,1)S(1)}, bf16[128,128]{1,0:T(8,128)(2,1)}, u32[]{:S(2)}) copy-start(bf16[128,128]{1,0:T(8,128)(2,1)} %slice.191) | copy-start | bytes 98308
  111.1 681.2 %copy-start.31 = (bf16[128,128]{1,0:T(8,128)(2,1)S(1)}, bf16[128,128]{1,0:T(8,128)(2,1)}, u32[]{:S(2)}) copy-start(bf16[128,128]{1,0:T(8,128)(2,1)} %slice.188) | copy-start | bytes 98308
  111.1 681.2 %copy-start.32 = (bf16[128,128]{1,0:T(8,128)(2,1)S(1)}, bf16[128,128]{1,0:T(8,128)(2,1)}, u32[]{:S(2)}) copy-start(bf16[128,128]{1,0:T(8,128)(2,1)} %slice.190) | copy-start | bytes 98308
  111.1 681.2 %copy-start.41 = (bf16[128,128]{1,0:T(8,128)(2,1)S(1)}, bf16[128,128]{1,0:T(8,128)(2,1)}, u32[]{:S(2)}) copy-start(bf16[128,128]{1,0:T(8,128)(2,1)} %neg.62) | copy-start | bytes 98308
  111.1 681.2 %copy-start.42 = (bf16[128,128]{1,0:T(8,128)(2,1)S(1)}, bf16[128,128]{1,0:T(8,128)(2,1)}, u32[]{:S(2)}) copy-start(bf16[128,128]{1,0:T(8,128)(2,1)} %neg.63) | copy-start | bytes 98308
  111.1 681.9 %copy-start.17 = (bf16[128,128]{1,0:T(8,128)(2,1)S(1)}, bf16[128,128]{1,0:T(8,128)(2,1)}, u32[]{:S(2)}) copy-start(bf16[128,128]{1,0:T(8,128)(2,1)} %slice.161) | copy-start | bytes 98308
  111.2 681.9 %copy-start.18 = (bf16[128,128]{1,0:T(8,128)(2,1)S(1)}, bf16[128,128]{1,0:T(8,128)(2,1)}, u32[]{:S(2)}) copy-start(bf16[128,128]{1,0:T(8,128)(2,1)} %slice.163) | copy-start | bytes 98308
  111.2 681.9 %copy-start.29 = (bf16[128,128]{1,0:T(8,128)(2,1)S(1)}, bf16[128,128]{1,0:T(8,128)(2,1)}, u32[]{:S(2)}) copy-start(bf16[128,128]{1,0:T(8,128)(2,1)} %slice.160) | copy-start | bytes 98308
  111.2 681.9 %copy-start.30 = (bf16[128,128]{1,0:T(8,128)(2,1)S(1)}, bf16[128,128]{1,0:T(8,128)(2,1)}, u32[]{:S(2)}) copy-start(bf16[128,128]{1,0:T(8,128)(2,1)} %slice.162) | copy-start | bytes 98308
  111.2 681.9 %copy-start.39 = (bf16[128,128]{1,0:T(8,128)(2,1)S(1)}, bf16[128,128]{1,0:T(8,128)(2,1)}, u32[]{:S(2)}) copy-start(bf16[128,128]{1,0:T(8,128)(2,1)} %neg.48) | copy-start | bytes 98308
  111.2 681.9 %copy-start.40 = (bf16[128,128]{1,0:T(8,128)(2,1)S(1)}, bf16[128,128]{1,0:T(8,128)(2,1)}, u32[]{:S(2)}) copy-start(bf16[128,128]{1,0:T(8,128)(2,1)} %neg.49) | copy-start | bytes 98308
  111.2 681.9 %copy-start.15 = (bf16[128,128]{1,0:T(8,128)(2,1)S(1)}, bf16[128,128]{1,0:T(8,128)(2,1)}, u32[]{:S(2)}) copy-start(bf16[128,128]{1,0:T(8,128)(2,1)} %slice.165) | copy-start | bytes 98308
  111.2 681.9 %copy-start.16 = (bf16[128,128]{1,0:T(8,128)(2,1)S(1)}, bf16[128,128]{1,0:T(8,128)(2,1)}, u32[]{:S(2)}) copy-start(bf16[128,128]{1,0:T(8,128)(2,1)} %slice.167) | copy-start | bytes 98308
  111.2 681.9 %copy-start.27 = (bf16[128,128]{1,0:T(8,128)(2,1)S(1)}, bf16[128,128]{1,0:T(8,128)(2,1)}, u32[]{:S(2)}) copy-start(bf16[128,128]{1,0:T(8,128)(2,1)} %slice.164) | copy-start | bytes 98308
  111.2 681.9 %copy-start.28 = (bf16[128,128]{1,0:T(8,128)(2,1)S(1)}, bf16[128,128]{1,0:T(8,128)(2,1)}, u32[]{:S(2)}) copy-start(bf16[128,128]{1,0:T(8,128)(2,1)} %slice.166) | copy-start | bytes 98308
  111.2 681.9 %copy-start.37 = (bf16[128,128]{1,0:T(8,128)(2,1)S(1)}, bf16[128,128]{1,0:T(8,128)(2,1)}, u32[]{:S(2)}) copy-start(bf16[128,128]{1,0:T(8,128)(2,1)} %neg.50) | copy-start | bytes 98308
  111.3 681.9 %copy-start.38 = (bf16[128,128]{1,0:T(8,128)(2,1)S(1)}, bf16[128,128]{1,0:T(8,128)(2,1)}, u32[]{:S(2)}) copy-start(bf16[128,128]{1,0:T(8,128)(2,1)} %neg.51) | copy-start | bytes 98308
  864.6 53.7 %copy-start.12 = (bf16[128,128]{1,0:T(8,128)(2,1)S(1)}, bf16[128,128]{1,0:T(8,128)(2,1)}, u32[]{:S(2)}) copy-start(bf16[128,128]{1,0:T(8,128)(2,1)} %slice.181) | copy-start | bytes 98308
  864.6 53.7 %copy-start.14 = (bf16[128,128]{1,0:T(8,128)(2,1)S(1)}, bf16[128,128]{1,0:T(8,128)(2,1)}, u32[]{:S(2)}) copy-start(bf16[128,128]{1,0:T(8,128)(2,1)} %slice.183) | copy-start | bytes 98308
  864.6 53.7 %copy-start.25 = (bf16[128,128]{1,0:T(8,128)(2,1)S(1)}, bf16[128,128]{1,0:T(8,128)(2,1)}, u32[]{:S(2)}) copy-start(bf16[128,128]{1,0:T(8,128)(2,1)} %slice.180) | copy-start | bytes 98308
  864.6 53.7 %copy-start.26 = (bf16[128,128]{1,0:T(8,128)(2,1)S(1)}, bf16[128,128]{1,0:T(8,128)(2,1)}, u32[]{:S(2)}) copy-start(bf16[128,128]{1,0:T(8,128)(2,1)} %slice.182) | copy-start | bytes 98308
  864.6 53.7 %copy-start.35 = (bf16[128,128]{1,0:T(8,128)(2,1)S(1)}, bf16[128,128]{1,0:T(8,128)(2,1)}, u32[]{:S(2)}) copy-start(bf16[128,128]{1,0:T(8,128)(2,1)} %neg.58) | copy-start | bytes 98308
  864.6 53.7 %copy-start.36 = (bf16[128,128]{1,0:T(8,128)(2,1)S(1)}, bf16[128,128]{1,0:T(8,128)(2,1)}, u32[]{:S(2)}) copy-start(bf16[128,128]{1,0:T(8,128)(2,1)} %neg.59) | copy-start | bytes 98308
  864.6 53.8 %copy-start.8 = (bf16[128,128]{1,0:T(8,128)(2,1)S(1)}, bf16[128,128]{1,0:T(8,128)(2,1)}, u32[]{:S(2)}) copy-start(bf16[128,128]{1,0:T(8,128)(2,1)} %slice.185) | copy-start | bytes 98308
  864.6 53.8 %copy-start.10 = (bf16[128,128]{1,0:T(8,128)(2,1)S(1)}, bf16[128,128]{1,0:T(8,128)(2,1)}, u32[]{:S(2)}) copy-start(bf16[128,128]{1,0:T(8,128)(2,1)} %slice.187) | copy-start | bytes 98308
  864.6 53.8 %copy-start.23 = (bf16[128,128]{1,0:T(8,128)(2,1)S(1)}, bf16[128,128]{1,0:T(8,128)(2,1)}, u32[]{:S(2)}) copy-start(bf16[128,128]{1,0:T(8,128)(2,1)} %slice.184) | copy-start | bytes 98308
  864.6 53.8 %copy-start.24 = (bf16[128,128]{1,0:T(8,128)(2,1)S(1)}, bf16[128,128]{1,0:T(8,128)(2,1)}, u32[]{:S(2)}) copy-start(bf16[128,128]{1,0:T(8,128)(2,1)} %slice.186) | copy-start | bytes 98308
  864.7 53.8 %copy-start.33 = (bf16[128,128]{1,0:T(8,128)(2,1)S(1)}, bf16[128,128]{1,0:T(8,128)(2,1)}, u32[]{:S(2)}) copy-start(bf16[128,128]{1,0:T(8,128)(2,1)} %neg.60) | copy-start | bytes 98308
  864.7 53.8 %copy-start.34 = (bf16[128,128]{1,0:T(8,128)(2,1)S(1)}, bf16[128,128]{1,0:T(8,128)(2,1)}, u32[]{:S(2)}) copy-start(bf16[128,128]{1,0:T(8,128)(2,1)} %neg.61) | copy-start | bytes 98308
  970.6 295.9 %reduce-scatter.5.cloned.1.call-start = ((), (), s32[]{:S(2)}) async-start(), calls=%async_computation.3 | async-start | bytes 4718592 | tf_op jit(solution)/shard_map/reduce_scatter | solution.py:462
  (13 other events, 197.2 us)
Sparse Core Ops, SparseCore 0:
  970.8 243.3 reduce-scatter.2
  1216.5 50.0 reduce-scatter.4

commit v2 on v1

--- a/solution.py
+++ b/solution.py
@@ -1,4 +1,6 @@
 import math
+
+import numpy as np
 
 import jax
 import jax.numpy as jnp
@@ -94,42 +96,40 @@
 MESH = pl.DeviceIdType.MESH
 
 
+def fixed_tables(length, direction):
+    indices = np.arange(length, dtype=np.int32)
+    phases = indices[:, None] * indices[None, :] % length
+    angles = phases.astype(np.float32) * np.float32(2.0 * math.pi / length)
+    factor = np.float32(1.0 / math.sqrt(length))
+    cosine, sine_part = np.cos(angles) * factor, np.float32(direction) * np.sin(angles) * factor
+    return cosine.astype(jnp.bfloat16), sine_part.astype(jnp.bfloat16)
+
+
 def rotation(cosine, sine_part, rows):
     if rows:
-        upper = jnp.concatenate([cosine, sine_part], axis=1)
-        lower = jnp.concatenate([-sine_part, cosine], axis=1)
-    else:
-        upper = jnp.concatenate([cosine, -sine_part], axis=1)
-        lower = jnp.concatenate([sine_part, cosine], axis=1)
-    return jnp.concatenate([upper, lower], axis=0)
+        return np.block([[cosine, sine_part], [-sine_part, cosine]])
+    return np.block([[cosine, -sine_part], [sine_part, cosine]])
 
 
 def plan_tables(slices, lines, readout, group):
-    eye = jnp.eye(group, dtype=jnp.bfloat16)
     quarter, half_y, half_z = readout // 4, lines // 2, slices // 2
-    cx, sx = dft_tables(readout, -1.0)
-    x_fwd = jnp.stack([rotation(cx[:quarter, r::4], sx[:quarter, r::4], True) for r in range(4)])
-    cx, sx = dft_tables(readout, 1.0)
-    x_inv = jnp.stack([rotation(cx[r::4, :quarter], sx[r::4, :quarter], True) for r in range(4)])
-    cy, sy = dft_tables(lines, -1.0)
-    y_fwd = jnp.stack([rotation(cy[p::2, :half_y], sy[p::2, :half_y], False) for p in range(2)])
-    cy, sy = dft_tables(lines, 1.0)
-    y_inv = jnp.stack([rotation(cy[:half_y, p::2], sy[:half_y, p::2], False) for p in range(2)])
-    cz, sz = dft_tables(slices, -1.0)
-    z_fwd = jnp.stack(
-        [
-            rotation(jnp.kron(cz[p::2, :half_z], eye), jnp.kron(sz[p::2, :half_z], eye), False)
-            for p in range(2)
-        ]
-    )
-    cz, sz = dft_tables(slices, 1.0)
-    z_inv = jnp.stack(
-        [
-            rotation(jnp.kron(cz[:half_z, p::2], eye), jnp.kron(sz[:half_z, p::2], eye), False)
-            for p in range(2)
-        ]
-    )
-    return x_fwd, x_inv, y_fwd, y_inv, z_fwd, z_inv
+
+    def wide(part):
+        return np.kron(part.astype(np.float32), np.eye(group, dtype=np.float32)).astype(part.dtype)
+
+    cx, sx = fixed_tables(readout, -1.0)
+    x_fwd = np.stack([rotation(cx[:quarter, r::4], sx[:quarter, r::4], True) for r in range(4)])
+    cx, sx = fixed_tables(readout, 1.0)
+    x_inv = np.stack([rotation(cx[r::4, :quarter], sx[r::4, :quarter], True) for r in range(4)])
+    cy, sy = fixed_tables(lines, -1.0)
+    y_fwd = np.stack([rotation(cy[p::2, :half_y], sy[p::2, :half_y], False) for p in range(2)])
+    cy, sy = fixed_tables(lines, 1.0)
+    y_inv = np.stack([rotation(cy[:half_y, p::2], sy[:half_y, p::2], False) for p in range(2)])
+    cz, sz = fixed_tables(slices, -1.0)
+    z_fwd = [rotation(wide(cz[p::2, :half_z]), wide(sz[p::2, :half_z]), False) for p in range(2)]
+    cz, sz = fixed_tables(slices, 1.0)
+    z_inv = [rotation(wide(cz[:half_z, p::2]), wide(sz[:half_z, p::2]), False) for p in range(2)]
+    return [jnp.asarray(t) for t in (x_fwd, x_inv, y_fwd, y_inv, np.stack(z_fwd), np.stack(z_inv))]
 
 
 def mm(left, right):
@@ -183,7 +183,8 @@
         u = parts[p].astype(jnp.bfloat16).reshape(flat, width)
         u = jnp.concatenate([u[:, :readout], u[:, readout:]], axis=0)
         k = mm(z_fwd[p], u)
-        m = mask_block[p].reshape(flat, readout).astype(jnp.float32)
+        m = mask_block[p].reshape(flat, readout // 4).astype(jnp.float32)
+        m = jnp.concatenate([m] * 4, axis=1)
         k = jnp.concatenate([k[:flat] * m, k[flat:] * m], axis=0).astype(jnp.bfloat16)
         back.append(mm(z_inv[p], k))
 
@@ -238,94 +239,18 @@
     return jnp.concatenate([image_ref[i % 2, 0, i // 2] for i in range(2 * chips)], axis=0)
 
 
-def forward_call(maps, image, x_fwd, y_fwd):
-    coils, slices, lines, width = maps.shape
-    chips, rows = image.shape[2], image.shape[3]
-    half = lines // 2
-
-    def body(map_ref, image_ref, x_ref, y_ref, out_ref):
-        even, odd = forward_body(map_ref[0, 0], image_rows(image_ref), x_ref[...], y_ref[...])
-        readout = even.shape[1]
-        out_ref[0, 0, :half, :readout] = even[:half]
-        out_ref[0, 0, :half, readout:] = even[half:]
-        out_ref[0, 0, half:, :readout] = odd[:half]
-        out_ref[0, 0, half:, readout:] = odd[half:]
-
-    return pl.pallas_call(
-        body,
-        grid=(slices, coils),
-        out_shape=jax.ShapeDtypeStruct(maps.shape, jnp.bfloat16),
-        in_specs=[
-            pl.BlockSpec((1, 1, lines, width), lambda z, j: (j, z, 0, 0)),
-            pl.BlockSpec((2, 1, chips, rows, width), lambda z, j: (0, z, 0, 0, 0)),
-            pl.BlockSpec(x_fwd.shape, lambda z, j: (0, 0, 0)),
-            pl.BlockSpec(y_fwd.shape, lambda z, j: (0, 0, 0)),
-        ],
-        out_specs=pl.BlockSpec((1, 1, lines, width), lambda z, j: (j, z, 0, 0)),
-        compiler_params=pltpu.CompilerParams(vmem_limit_bytes=48 << 20),
-        name="forward_xy",
-    )(maps, image, x_fwd, y_fwd)
-
-
-def slab_call(volume, mask, z_fwd, z_inv, group):
-    coils, slices, lines, width = volume.shape
-    half = slices // 2
-
-    def body(block_ref, mask_ref, f_ref, b_ref, out_ref):
-        low, high = slab_body(block_ref[0], mask_ref[...], f_ref[...], b_ref[...])
-        out_ref[0, :half] = low
-        out_ref[0, half:] = high
-
-    return pl.pallas_call(
-        body,
-        grid=(lines // group, coils),
-        out_shape=jax.ShapeDtypeStruct(volume.shape, jnp.bfloat16),
-        in_specs=[
-            pl.BlockSpec((1, slices, group, width), lambda y, j: (j, 0, y, 0)),
-            pl.BlockSpec((2, half, group, width // 2), lambda y, j: (0, 0, y, 0)),
-            pl.BlockSpec(z_fwd.shape, lambda y, j: (0, 0, 0)),
-            pl.BlockSpec(z_inv.shape, lambda y, j: (0, 0, 0)),
-        ],
-        out_specs=pl.BlockSpec((1, slices, group, width), lambda y, j: (j, 0, y, 0)),
-        compiler_params=pltpu.CompilerParams(vmem_limit_bytes=48 << 20),
-        name="slab_mask",
-    )(volume, mask, z_fwd, z_inv)
-
-
-def backward_call(volume, maps, x_inv, y_inv):
-    coils, slices, lines, width = volume.shape
-
-    def body(block_ref, map_ref, x_ref, y_ref, out_ref):
-        total = backward_body(block_ref[0, 0], map_ref[0, 0], x_ref[...], y_ref[...])
-        for j in range(1, coils):
-            total += backward_body(block_ref[j, 0], map_ref[j, 0], x_ref[...], y_ref[...])
-        out_ref[0] = total.astype(out_ref.dtype)
-
-    return pl.pallas_call(
-        body,
-        grid=(slices,),
-        out_shape=jax.ShapeDtypeStruct((slices, lines, width), jnp.bfloat16),
-        in_specs=[
-            pl.BlockSpec((coils, 1, lines, width), lambda z: (0, z, 0, 0)),
-            pl.BlockSpec((coils, 1, lines, width), lambda z: (0, z, 0, 0)),
-            pl.BlockSpec(x_inv.shape, lambda z: (0, 0, 0)),
-            pl.BlockSpec(y_inv.shape, lambda z: (0, 0, 0)),
-        ],
-        out_specs=pl.BlockSpec((1, lines, width), lambda z: (z, 0, 0)),
-        compiler_params=pltpu.CompilerParams(vmem_limit_bytes=56 << 20),
-        name="backward_yx",
-    )(volume, maps, x_inv, y_inv)
-
-
-def exchange_call(coil_maps, object_image):
+def exchange_call(coil_maps, object_image, mask, x_fwd, y_fwd, z_fwd, z_inv, group):
     pencils, columns = lax.axis_size("pencil"), lax.axis_size("coil")
     coils, slices, rows, width = coil_maps.shape
     per, chips, share = coils // pencils, pencils // 2, slices // columns
+    lines, readout = rows * pencils, width // 2
+    half_y, half_z = lines // 2, slices // 2
     shifts = sorted(range(1, pencils), key=lambda s: abs(s - pencils // 2))
 
     def kernel(
-        map_ref, image_ref, out_ref, full_ref, own_sem, map_send, map_recv, im_send, im_recv,
-        col_send, col_recv, core_send, core_recv,
+        map_ref, image_ref, mask_ref, xf_ref, yf_ref, zf_ref, zi_ref,
+        out_ref, full_ref, mid_ref, vol_ref,
+        own_sem, map_send, map_recv, im_send, im_recv, col_send, col_recv, core_send, core_recv,
     ):
         me, column = lax.axis_index("pencil"), lax.axis_index("coil")
         chip, core = me // 2, me % 2
@@ -342,60 +267,56 @@
         pl.semaphore_wait(barrier, pencils + columns - 2)
 
         quarter = pl.ds(column * share, share)
+        own_image = pltpu.make_async_copy(
+            image_ref.at[quarter], full_ref.at[core, quarter, chip], own_sem.at[per]
+        )
         own = [
             pltpu.make_async_copy(
-                image_ref.at[quarter], full_ref.at[core, quarter, chip], own_sem.at[per]
-            )
+                map_ref.at[me * per + j], out_ref.at[j, :, pl.ds(me * rows, rows)], own_sem.at[j]
+            )
+            for j in range(per)
         ]
-        for j in range(per):
-            own.append(
-                pltpu.make_async_copy(
-                    map_ref.at[me * per + j], out_ref.at[j, :, pl.ds(me * rows, rows)], own_sem.at[j]
-                )
-            )
-        along = []
-        for i, s in enumerate(range(1, chips)):
-            along.append(
+        along = [
+            pltpu.make_async_remote_copy(
+                src_ref=image_ref.at[quarter],
+                dst_ref=full_ref.at[core, quarter, chip],
+                send_sem=im_send.at[s - 1],
+                recv_sem=im_recv.at[s - 1],
+                device_id=(column, lax.rem(me + 2 * s, pencils)),
+                device_id_type=MESH,
+            )
+            for s in range(1, chips)
+        ]
+        moves = [
+            [
                 pltpu.make_async_remote_copy(
-                    src_ref=image_ref.at[quarter],
-                    dst_ref=full_ref.at[core, quarter, chip],
-                    send_sem=im_send.at[i],
-                    recv_sem=im_recv.at[i],
-                    device_id=(column, lax.rem(me + 2 * s, pencils)),
+                    src_ref=map_ref.at[lax.rem(me + s, pencils) * per + j],
+                    dst_ref=out_ref.at[j, :, pl.ds(me * rows, rows)],
+                    send_sem=map_send.at[j, i],
+                    recv_sem=map_recv.at[j, i],
+                    device_id=(column, lax.rem(me + s, pencils)),
                     device_id_type=MESH,
                 )
-            )
-        moves = []
-        for j in range(per):
-            for i, s in enumerate(shifts):
-                target = lax.rem(me + s, pencils)
-                moves.append(
-                    pltpu.make_async_remote_copy(
-                        src_ref=map_ref.at[target * per + j],
-                        dst_ref=out_ref.at[j, :, pl.ds(me * rows, rows)],
-                        send_sem=map_send.at[j, i],
-                        recv_sem=map_recv.at[j, i],
-                        device_id=(column, target),
-                        device_id_type=MESH,
-                    )
-                )
-        for copy in along + moves + own:
+                for i, s in enumerate(shifts)
+            ]
+            for j in range(per)
+        ]
+        for copy in along + moves[0] + [own_image] + own:
             copy.start()
-        own[0].wait()
+        own_image.wait()
         for copy in along:
             copy.wait()
-        across = []
-        for i, s in enumerate(range(1, columns)):
-            across.append(
-                pltpu.make_async_remote_copy(
-                    src_ref=full_ref.at[core, quarter],
-                    dst_ref=full_ref.at[core, quarter],
-                    send_sem=col_send.at[i],
-                    recv_sem=col_recv.at[i],
-                    device_id=(lax.rem(column + s, columns), me),
-                    device_id_type=MESH,
-                )
-            )
+        across = [
+            pltpu.make_async_remote_copy(
+                src_ref=full_ref.at[core, quarter],
+                dst_ref=full_ref.at[core, quarter],
+                send_sem=col_send.at[s - 1],
+                recv_sem=col_recv.at[s - 1],
+                device_id=(lax.rem(column + s, columns), me),
+                device_id_type=MESH,
+            )
+            for s in range(1, columns)
+        ]
         for copy in across:
             copy.start()
         for copy in across:
@@ -410,19 +331,52 @@
         )
         pair.start()
         pair.wait()
-        for copy in own[1:] + moves:
-            copy.wait()
+
+        def forward(map_block, image_block, o_ref):
+            even, odd = forward_body(map_block[0], image_rows(image_block), xf_ref, yf_ref)
+            o_ref[0, :half_y, :readout] = even[:half_y]
+            o_ref[0, :half_y, readout:] = even[half_y:]
+            o_ref[0, half_y:, :readout] = odd[:half_y]
+            o_ref[0, half_y:, readout:] = odd[half_y:]
+
+        def slab(block, mask_block, o_ref):
+            low, high = slab_body(block[...], mask_block[...], zf_ref, zi_ref)
+            o_ref[:half_z] = low
+            o_ref[half_z:] = high
+
+        plane = pl.BlockSpec((1, lines, width), lambda z: (z, 0, 0))
+        image_spec = pl.BlockSpec((2, 1, chips, rows, width), lambda z: (0, z, 0, 0, 0))
+        slab_spec = pl.BlockSpec((slices, group, width), lambda y: (0, y, 0))
+        mask_spec = pl.BlockSpec((2, half_z, group, readout // 4), lambda y: (0, 0, y, 0))
+        for j in range(per):
+            for i in range(len(shifts)):
+                moves[j][i].wait_send()
+                if j + 1 < per:
+                    moves[j + 1][i].start()
+            for copy in moves[j]:
+                copy.wait_recv()
+            own[j].wait()
+            pltpu.emit_pipeline(
+                forward, grid=(slices,), in_specs=[plane, image_spec], out_specs=[plane]
+            )(out_ref.at[j], full_ref, mid_ref.at[j])
+            pltpu.emit_pipeline(
+                slab, grid=(lines // group,), in_specs=[slab_spec, mask_spec], out_specs=[slab_spec]
+            )(mid_ref.at[j], mask_ref, vol_ref.at[j])
 
     dma = pltpu.SemaphoreType.DMA
     anywhere = pl.BlockSpec(memory_space=pl.ANY)
+    vmem = pl.BlockSpec(memory_space=pltpu.VMEM)
+    whole = jax.ShapeDtypeStruct((per, slices, lines, width), jnp.bfloat16)
     return pl.pallas_call(
         kernel,
         out_shape=[
-            jax.ShapeDtypeStruct((per, slices, rows * pencils, width), jnp.bfloat16),
+            whole,
             jax.ShapeDtypeStruct((2, slices, chips, rows, width), jnp.bfloat16),
+            whole,
+            whole,
         ],
-        in_specs=[anywhere, anywhere],
-        out_specs=[anywhere, anywhere],
+        in_specs=[anywhere, anywhere, anywhere, vmem, vmem, vmem, vmem],
+        out_specs=[anywhere] * 4,
         scratch_shapes=[
             dma((per + 1,)),
             dma((per, pencils - 1)),
@@ -434,9 +388,177 @@
             dma,
             dma,
         ],
-        compiler_params=pltpu.CompilerParams(collective_id=0, has_side_effects=True),
-        name="exchange_maps",
-    )(coil_maps, object_image)
+        compiler_params=pltpu.CompilerParams(
+            collective_id=0, has_side_effects=True, vmem_limit_bytes=56 << 20
+        ),
+        name="exchange_forward",
+    )(coil_maps, object_image, mask, x_fwd, y_fwd, z_fwd, z_inv)
+
+
+def combine_call(volume, maps, x_inv, y_inv):
+    pencils, columns = lax.axis_size("pencil"), lax.axis_size("coil")
+    per, slices, lines, width = volume.shape
+    rows, chips, share = lines // pencils, pencils // 2, slices // columns
+    volume = volume.reshape(per, columns, share, lines, width)
+    maps = maps.reshape(per, columns, share, lines, width)
+
+    def kernel(
+        vol_ref, map_ref, xi_ref, yi_ref, part_ref, out_ref,
+        mine, from_core, from_column, column_sum, from_chip,
+        own_sem, core_send, core_recv, col_send, col_recv, chip_send, chip_recv,
+    ):
+        me, column = lax.axis_index("pencil"), lax.axis_index("coil")
+        chip, core = me // 2, me % 2
+
+        barrier = pltpu.get_barrier_semaphore()
+        pl.semaphore_signal(barrier, device_id=(column, me + 1 - 2 * core), device_id_type=MESH)
+        for s in range(1, columns):
+            pl.semaphore_signal(
+                barrier, device_id=(lax.rem(column + s, columns), me), device_id_type=MESH
+            )
+        for s in range(1, chips):
+            pl.semaphore_signal(
+                barrier, device_id=(column, lax.rem(me + 2 * s, pencils)), device_id_type=MESH
+            )
+        pl.semaphore_wait(barrier, columns + chips - 1)
+
+        def own_copy(k):
+            return pltpu.make_async_copy(part_ref.at[k, core], mine.at[k], own_sem.at[k])
+
+        def core_copy(k):
+            return pltpu.make_async_remote_copy(
+                src_ref=part_ref.at[k, 1 - core],
+                dst_ref=from_core.at[k],
+                send_sem=core_send.at[k],
+                recv_sem=core_recv.at[k],
+                device_id=(column, me + 1 - 2 * core),
+                device_id_type=MESH,
+            )
+
+        def column_copy(k, s):
+            target = lax.rem(column + s, columns)
+            return pltpu.make_async_remote_copy(
+                src_ref=mine.at[k, target],
+                dst_ref=from_column.at[k, s - 1],
+                send_sem=col_send.at[k, s - 1],
+                recv_sem=col_recv.at[k, s - 1],
+                device_id=(target, me),
+                device_id_type=MESH,
+            )
+
+        def chip_copy(k, s):
+            target = lax.rem(chip + s, chips)
+            return pltpu.make_async_remote_copy(
+                src_ref=column_sum.at[k, target],
+                dst_ref=from_chip.at[k, s - 1],
+                send_sem=chip_send.at[k, s - 1],
+                recv_sem=chip_recv.at[k, s - 1],
+                device_id=(column, 2 * target + core),
+                device_id_type=MESH,
+            )
+
+        def backward(block, map_block, o_ref):
+            total = backward_body(block[0, 0], map_block[0, 0], xi_ref, yi_ref)
+            for j in range(1, per):
+                total += backward_body(block[j, 0], map_block[j, 0], xi_ref, yi_ref)
+            total = total.astype(o_ref.dtype)
+            for i in range(pencils):
+                o_ref[i % 2, 0, i // 2] = total[i * rows : (i + 1) * rows]
+
+        plane = pl.BlockSpec((per, 1, lines, width), lambda c: (0, c, 0, 0))
+        part_spec = pl.BlockSpec((2, 1, chips, rows, width), lambda c: (0, c, 0, 0, 0))
+
+        def step(t, carry):
+            @pl.when(t < share)
+            def _():
+                pltpu.emit_pipeline(
+                    backward, grid=(columns,), in_specs=[plane, plane], out_specs=[part_spec]
+                )(vol_ref.at[:, :, t], map_ref.at[:, :, t], part_ref.at[t])
+                core_copy(t).start()
+                own_copy(t).start()
+
+            @pl.when((t >= 1) & (t < share + 1))
+            def _():
+                k = t - 1
+                own_copy(k).wait()
+                core_copy(k).wait_recv()
+                for c in range(columns):
+                    for z in range(chips):
+                        mine[k, c, z] = (
+                            mine[k, c, z].astype(jnp.float32)
+                            + from_core[k, c, z].astype(jnp.float32)
+                        ).astype(jnp.bfloat16)
+                for s in range(1, columns):
+                    column_copy(k, s).start()
+
+            @pl.when((t >= 2) & (t < share + 2))
+            def _():
+                k = t - 2
+                for s in range(1, columns):
+                    column_copy(k, s).wait_recv()
+                for z in range(chips):
+                    total = mine[k, column, z].astype(jnp.float32)
+                    for s in range(1, columns):
+                        total += from_column[k, s - 1, z].astype(jnp.float32)
+                    column_sum[k, z] = total.astype(jnp.bfloat16)
+                for s in range(1, chips):
+                    chip_copy(k, s).start()
+
+            @pl.when(t >= 3)
+            def _():
+                k = t - 3
+                for s in range(1, chips):
+                    chip_copy(k, s).wait_recv()
+                total = column_sum[k, chip].astype(jnp.float32)
+                for s in range(1, chips):
+                    total += from_chip[k, s - 1].astype(jnp.float32)
+                out_ref[k] = total
+
+            return carry
+
+        lax.fori_loop(0, share + 3, step, 0)
+
+        def finish(k, carry):
+            core_copy(k).wait_send()
+            for s in range(1, columns):
+                column_copy(k, s).wait_send()
+            for s in range(1, chips):
+                chip_copy(k, s).wait_send()
+            return carry
+
+        lax.fori_loop(0, share, finish, 0)
+
+    dma = pltpu.SemaphoreType.DMA
+    anywhere = pl.BlockSpec(memory_space=pl.ANY)
+    vmem = pl.BlockSpec(memory_space=pltpu.VMEM)
+    block = (chips, rows, width)
+    return pl.pallas_call(
+        kernel,
+        out_shape=[
+            jax.ShapeDtypeStruct((share, 2, columns) + block, jnp.bfloat16),
+            jax.ShapeDtypeStruct((share, rows, width), jnp.float32),
+        ],
+        in_specs=[anywhere, anywhere, vmem, vmem],
+        out_specs=[anywhere, vmem],
+        scratch_shapes=[
+            pltpu.VMEM((share, columns) + block, jnp.bfloat16),
+            pltpu.VMEM((share, columns) + block, jnp.bfloat16),
+            pltpu.VMEM((share, columns - 1) + block, jnp.bfloat16),
+            pltpu.VMEM((share,) + block, jnp.bfloat16),
+            pltpu.VMEM((share, chips - 1, rows, width), jnp.bfloat16),
+            dma((share,)),
+            dma((share,)),
+            dma((share,)),
+            dma((share, columns - 1)),
+            dma((share, columns - 1)),
+            dma((share, chips - 1)),
+            dma((share, chips - 1)),
+        ],
+        compiler_params=pltpu.CompilerParams(
+            collective_id=1, has_side_effects=True, vmem_limit_bytes=60 << 20
+        ),
+        name="backward_combine",
+    )(volume, maps, x_inv, y_inv)[1]
 
 
 def plan_mask(sample_mask, readout):
@@ -444,7 +566,7 @@
     run = readout // segments // 4
     flags = sample_mask.reshape(slices // 2, 2, lines // 2, 2, segments).transpose(1, 0, 3, 2, 4)
     flags = (flags > 0).astype(jnp.bfloat16).reshape(2, slices // 2, lines, segments)
-    return jnp.tile(jnp.repeat(flags, run, axis=3), (1, 1, 1, 4))
+    return jnp.repeat(flags, run, axis=3)
 
 
 def whole_coils(object_image, coil_maps, sample_mask):
@@ -454,14 +576,10 @@
     group = 16
     x_fwd, x_inv, y_fwd, y_inv, z_fwd, z_inv = plan_tables(slices, lines, readout, group)
     mask = plan_mask(sample_mask, readout)
-    maps, image = exchange_call(coil_maps, object_image)
-    volume = forward_call(maps, image, x_fwd, y_fwd)
-    volume = slab_call(volume, mask, z_fwd, z_inv, group)
-    partial_sum = backward_call(volume, maps, x_inv, y_inv)
-    partial_sum = lax.psum_scatter(partial_sum, "coil", scatter_dimension=0, tiled=True)
-    return lax.psum_scatter(partial_sum, "pencil", scatter_dimension=1, tiled=True).astype(
-        jnp.float32
+    maps, _, _, volume = exchange_call(
+        coil_maps, object_image, mask, x_fwd, y_fwd, z_fwd, z_inv, group
     )
+    return combine_call(volume, maps, x_inv, y_inv)
 
 
 def solution(mesh):

time: 1280 us -> 969 us (0.76)
  waiting for transfers between devices: 296 us -> 0 us
  Pallas kernels: 857 us -> 956 us
  local copies, waits for them, and re-layouts: 70.4 us -> 7.3 us
  other arithmetic: 37.9 us -> 0.94 us
  between operations: 14.2 us -> 0.05 us
    reduce_scatter x2 -> x0, waiting for transfers between devices: 296 us -> none  [the longest x1 244 us: whole_coils(): lax.psum_scatter(partial_sum, 'coil', scatter_dimension=0, tiled=True)]
    pallas_call x4 -> x2, Pallas kernels: 857 us -> 956 us  [the longest x1 771 us: exchange_call(): pl.pallas_call(kernel, out_shape=[whole, jax.ShapeDtypeStruct((2, slices,...]
    slice x32 -> x0, local copies, waits for them, and re-layouts: 29.4 us -> none  [the longest x4 7.02 us: plan_tables(): cx[:quarter, r::4]]
    another operation x3 -> x0, local copies, waits for them, and re-layouts: 21.7 us -> none  [plan_mask(): return jnp.tile(jnp.repeat(flags, run, axis=3), (1, 1, 1, 4))]
    convert_element_type x11 -> x0, other arithmetic: 17.3 us -> none  [the longest x6 10.1 us: dft_tables(): sine_part = (direction * jnp.sin(angles) * factor).astype(jnp.bfloat16)]
    mul x8 -> x0, local copies, waits for them, and re-layouts: 15.3 us -> none  [the longest x2 5.65 us: plan_tables(): jnp.kron(cz[p::2, :half_z], eye)]
    neg x16 -> x0, other arithmetic: 14 us -> none  [the longest x8 7.92 us: rotation(): lower = jnp.concatenate([-sine_part, cosine], axis=1)]
  transfers between devices with their start and end apart: 2 -> 0, of which waited for: 2 -> 0; matrix products, arithmetic and copies ran while one was open for 0% -> 0% of each run, Pallas kernels for 0% -> 0%
where the time goes in v2:
time: 969 us; the launch traced here: 965 us
  Pallas kernels  956 us (99%)
    pallas_call x1, Pallas kernels, exchange_call(): pl.pallas_call(kernel, out_shape=[whole, jax.ShapeDtypeStruct((2, slices,...  771 us
    pallas_call x1, Pallas kernels, combine_call(): pl.pallas_call(kernel, out_shape=[jax.ShapeDtypeStruct((share, 2, columns...  186 us

profile of v2, /device:TPU:0, one launch (start us, length us, event | category | flops | bytes accessed | tf_op | source)
XLA Modules:
  0.0 964.7 jit_solution(17888084802110811215)
XLA Ops:
  0.0 0.9 compare_convert_fusion
  0.9 1.1 copy.10
  2.0 1.3 copy.14
  3.4 0.2 broadcast_in_dim.3
  3.6 2.4 copy.13.mask_ref
  6.0 770.6 %exchange_forward.1 = (bf16[2,32,256,1024]{3,2,1,0:T(8,128)(2,1)}, bf16[2,32,4,32,1024]{4,3,2,1,0:T(8,128)(2,1)}, bf16[2,32,256,1024]{3,2,1,0:T(8,128)(2,1)}, bf16[2,32,256,1024]{3,2,1,0:T(8,128)(2,1)}) custom-call(bf16[16,32,32,1024]{3,2,1,0:T(8,128)(2,1)} %map_ref.1, bf16[32,32,1024]{2,1,0:T(8,128)(2,1)} %image_ref.1, ...), custom_call_target="tpu_custom_call" | custom-call | tf_op jit(solution)/shard_map/exchange_forward/pallas_call | solution.py:370
  776.5 185.9 %backward_combine.1 = (bf16[8,2,4,4,32,1024]{5,4,3,2,1,0:T(8,128)(2,1)}, f32[8,32,1024]{2,1,0:T(8,128)}) custom-call(bf16[2,4,8,256,1024]{4,3,2,1,0:T(8,128)(2,1)} %bitcast.9, bf16[2,4,8,256,1024]{4,3,2,1,0:T(8,128)(2,1)} %bitcast.8, bf16[4,256,256]{2,1,0:T(8,128)(2,1)} %constant.15.clone.xi_ref, bf16[2,256,256]{2,1,0:T(8,128)(2,1)} %constant.17.clone.yi_ref), custom_call_target="tpu_custom_call" | custom-call | tf_op jit(solution)/shard_map/backward_combine/pallas_call | solution.py:535
  962.4 2.3 copy.17
  (1 shorter events, 0.0 us)

commit v3 on v2

--- a/solution.py
+++ b/solution.py
@@ -239,18 +239,28 @@
     return jnp.concatenate([image_ref[i % 2, 0, i // 2] for i in range(2 * chips)], axis=0)
 
 
-def exchange_call(coil_maps, object_image, mask, x_fwd, y_fwd, z_fwd, z_inv, group):
+def flip(value, bits):
+    bit = 1
+    while bit <= bits:
+        if bits & bit:
+            value = value + bit - 2 * bit * ((value // bit) % 2)
+        bit *= 2
+    return value
+
+
+def exchange_call(coil_maps, object_image, mask, tables, group, pieces):
     pencils, columns = lax.axis_size("pencil"), lax.axis_size("coil")
     coils, slices, rows, width = coil_maps.shape
     per, chips, share = coils // pencils, pencils // 2, slices // columns
     lines, readout = rows * pencils, width // 2
     half_y, half_z = lines // 2, slices // 2
     shifts = sorted(range(1, pencils), key=lambda s: abs(s - pencils // 2))
+    last, run = per - 1, slices // pieces
 
     def kernel(
-        map_ref, image_ref, mask_ref, xf_ref, yf_ref, zf_ref, zi_ref,
-        out_ref, full_ref, mid_ref, vol_ref,
-        own_sem, map_send, map_recv, im_send, im_recv, col_send, col_recv, core_send, core_recv,
+        map_ref, image_ref, mask_ref, xf_ref, xi_ref, yf_ref, yi_ref, zf_ref, zi_ref,
+        out_ref, full_ref, mid_ref, vol_ref, part_ref,
+        own_sem, map_send, map_recv, end_send, end_recv, im_send, im_recv, col_send, col_recv, core_send, core_recv,
     ):
         me, column = lax.axis_index("pencil"), lax.axis_index("coil")
         chip, core = me // 2, me % 2
@@ -275,17 +285,6 @@
                 map_ref.at[me * per + j], out_ref.at[j, :, pl.ds(me * rows, rows)], own_sem.at[j]
             )
             for j in range(per)
-        ]
-        along = [
-            pltpu.make_async_remote_copy(
-                src_ref=image_ref.at[quarter],
-                dst_ref=full_ref.at[core, quarter, chip],
-                send_sem=im_send.at[s - 1],
-                recv_sem=im_recv.at[s - 1],
-                device_id=(column, lax.rem(me + 2 * s, pencils)),
-                device_id_type=MESH,
-            )
-            for s in range(1, chips)
         ]
         moves = [
             [
@@ -299,13 +298,49 @@
                 )
                 for i, s in enumerate(shifts)
             ]
-            for j in range(per)
+            for j in range(last)
         ]
-        for copy in along + moves[0] + [own_image] + own:
-            copy.start()
+        ends = [
+            [
+                pltpu.make_async_remote_copy(
+                    src_ref=map_ref.at[
+                        lax.rem(me + s, pencils) * per + last, pl.ds(g * run, run)
+                    ],
+                    dst_ref=out_ref.at[last, pl.ds(g * run, run), pl.ds(me * rows, rows)],
+                    send_sem=end_send.at[g, i],
+                    recv_sem=end_recv.at[g, i],
+                    device_id=(column, lax.rem(me + s, pencils)),
+                    device_id_type=MESH,
+                )
+                for i, s in enumerate(shifts)
+            ]
+            for g in range(pieces)
+        ]
+
+        def along(d, n, h):
+            block = full_ref.at[core, quarter, flip(chip, h)]
+            return pltpu.make_async_remote_copy(
+                src_ref=block,
+                dst_ref=block,
+                send_sem=im_send.at[n],
+                recv_sem=im_recv.at[n],
+                device_id=(column, 2 * flip(chip, d) + core),
+                device_id_type=MESH,
+            )
+
+        own_image.start()
         own_image.wait()
-        for copy in along:
-            copy.wait()
+        held, d, first = [0], chips // 2, True
+        while d >= 1:
+            copies = [along(d, len(held) - 1 + n, h) for n, h in enumerate(held)]
+            for copy in copies:
+                copy.start()
+            if first:
+                for copy in moves[0] + own:
+                    copy.start()
+            for copy in copies:
+                copy.wait()
+            held, d, first = held + [h ^ d for h in held], d // 2, False
         across = [
             pltpu.make_async_remote_copy(
                 src_ref=full_ref.at[core, quarter],
@@ -348,20 +383,52 @@
         image_spec = pl.BlockSpec((2, 1, chips, rows, width), lambda z: (0, z, 0, 0, 0))
         slab_spec = pl.BlockSpec((slices, group, width), lambda y: (0, y, 0))
         mask_spec = pl.BlockSpec((2, half_z, group, readout // 4), lambda y: (0, 0, y, 0))
-        for j in range(per):
+        part_spec = pl.BlockSpec(
+            (1, 2, 1, chips, rows, width), lambda k, c: (k, 0, c, 0, 0, 0)
+        )
+        strided = pl.BlockSpec((1, lines, width), lambda k, c: (c * share + k, 0, 0))
+
+        def backward(block, map_block, o_ref):
+            total = backward_body(block[0], map_block[0], xi_ref, yi_ref).astype(o_ref.dtype)
+            for i in range(pencils):
+                o_ref[0, i % 2, 0, i // 2] = total[i * rows : (i + 1) * rows]
+
+        def slabs(j):
+            pltpu.emit_pipeline(
+                slab, grid=(lines // group,), in_specs=[slab_spec, mask_spec], out_specs=[slab_spec]
+            )(mid_ref.at[j], mask_ref, vol_ref.at[j])
+
+        for j in range(last):
             for i in range(len(shifts)):
                 moves[j][i].wait_send()
-                if j + 1 < per:
+                if j + 1 < last:
                     moves[j + 1][i].start()
+                else:
+                    ends[0][i].start()
+                    ends[1][i].start()
             for copy in moves[j]:
                 copy.wait_recv()
             own[j].wait()
             pltpu.emit_pipeline(
                 forward, grid=(slices,), in_specs=[plane, image_spec], out_specs=[plane]
             )(out_ref.at[j], full_ref, mid_ref.at[j])
+            slabs(j)
             pltpu.emit_pipeline(
-                slab, grid=(lines // group,), in_specs=[slab_spec, mask_spec], out_specs=[slab_spec]
-            )(mid_ref.at[j], mask_ref, vol_ref.at[j])
+                backward, grid=(share, columns), in_specs=[strided, strided], out_specs=[part_spec]
+            )(vol_ref.at[j], out_ref.at[j], part_ref.at[j])
+        own[last].wait()
+        for g in range(pieces):
+            for i in range(len(shifts)):
+                ends[g][i].wait_send()
+                if g + 2 < pieces:
+                    ends[g + 2][i].start()
+            for copy in ends[g]:
+                copy.wait_recv()
+            piece = pl.ds(g * run, run)
+            pltpu.emit_pipeline(
+                forward, grid=(run,), in_specs=[plane, image_spec], out_specs=[plane]
+            )(out_ref.at[last, piece], full_ref.at[:, piece], mid_ref.at[last, piece])
+        slabs(last)
 
     dma = pltpu.SemaphoreType.DMA
     anywhere = pl.BlockSpec(memory_space=pl.ANY)
@@ -374,13 +441,16 @@
             jax.ShapeDtypeStruct((2, slices, chips, rows, width), jnp.bfloat16),
             whole,
             whole,
+            jax.ShapeDtypeStruct((last, share, 2, columns, chips, rows, width), jnp.bfloat16),
         ],
-        in_specs=[anywhere, anywhere, anywhere, vmem, vmem, vmem, vmem],
-        out_specs=[anywhere] * 4,
+        in_specs=[anywhere] * 3 + [vmem] * 6,
+        out_specs=[anywhere] * 5,
         scratch_shapes=[
             dma((per + 1,)),
-            dma((per, pencils - 1)),
-            dma((per, pencils - 1)),
+            dma((last, pencils - 1)),
+            dma((last, pencils - 1)),
+            dma((pieces, pencils - 1)),
+            dma((pieces, pencils - 1)),
             dma((chips - 1,)),
             dma((chips - 1,)),
             dma((columns - 1,)),
@@ -392,35 +462,33 @@
             collective_id=0, has_side_effects=True, vmem_limit_bytes=56 << 20
         ),
         name="exchange_forward",
-    )(coil_maps, object_image, mask, x_fwd, y_fwd, z_fwd, z_inv)
-
-
-def combine_call(volume, maps, x_inv, y_inv):
+    )(coil_maps, object_image, mask, *tables)
+
+
+def combine_call(volume, maps, parts, x_inv, y_inv):
     pencils, columns = lax.axis_size("pencil"), lax.axis_size("coil")
     per, slices, lines, width = volume.shape
-    rows, chips, share = lines // pencils, pencils // 2, slices // columns
+    rows, chips, share, last = lines // pencils, pencils // 2, slices // columns, per - 1
     volume = volume.reshape(per, columns, share, lines, width)
     maps = maps.reshape(per, columns, share, lines, width)
 
     def kernel(
-        vol_ref, map_ref, xi_ref, yi_ref, part_ref, out_ref,
-        mine, from_core, from_column, column_sum, from_chip,
-        own_sem, core_send, core_recv, col_send, col_recv, chip_send, chip_recv,
+        vol_ref, map_ref, early_ref, xi_ref, yi_ref, part_ref, out_ref,
+        mine, from_core, from_first, from_second, column_sum, from_chip,
+        own_sem, core_send, core_recv, one_send, one_recv, two_send, two_recv, chip_send, chip_recv,
     ):
         me, column = lax.axis_index("pencil"), lax.axis_index("coil")
         chip, core = me // 2, me % 2
 
         barrier = pltpu.get_barrier_semaphore()
         pl.semaphore_signal(barrier, device_id=(column, me + 1 - 2 * core), device_id_type=MESH)
-        for s in range(1, columns):
-            pl.semaphore_signal(
-                barrier, device_id=(lax.rem(column + s, columns), me), device_id_type=MESH
-            )
+        for bit in (1, 2):
+            pl.semaphore_signal(barrier, device_id=(flip(column, bit), me), device_id_type=MESH)
         for s in range(1, chips):
             pl.semaphore_signal(
                 barrier, device_id=(column, lax.rem(me + 2 * s, pencils)), device_id_type=MESH
             )
-        pl.semaphore_wait(barrier, columns + chips - 1)
+        pl.semaphore_wait(barrier, chips + 2)
 
         def own_copy(k):
             return pltpu.make_async_copy(part_ref.at[k, core], mine.at[k], own_sem.at[k])
@@ -435,13 +503,26 @@
                 device_id_type=MESH,
             )
 
-        def column_copy(k, s):
-            target = lax.rem(column + s, columns)
+        side = [pl.ds(h * (chips // 2), chips // 2) for h in range(2)]
+
+        def one_copy(k, h, n):
+            target = flip(column, 1 + h)
             return pltpu.make_async_remote_copy(
-                src_ref=mine.at[k, target],
-                dst_ref=from_column.at[k, s - 1],
-                send_sem=col_send.at[k, s - 1],
-                recv_sem=col_recv.at[k, s - 1],
+                src_ref=mine.at[k, flip(column, 3) if n else target, side[h]],
+                dst_ref=from_first.at[k, h, n],
+                send_sem=one_send.at[k, 2 * h + n],
+                recv_sem=one_recv.at[k, 2 * h + n],
+                device_id=(target, me),
+                device_id_type=MESH,
+            )
+
+        def two_copy(k, h):
+            target = flip(column, 2 - h)
+            return pltpu.make_async_remote_copy(
+                src_ref=mine.at[k, target, side[h]],
+                dst_ref=from_second.at[k, h],
+                send_sem=two_send.at[k, h],
+                recv_sem=two_recv.at[k, h],
                 device_id=(target, me),
                 device_id_type=MESH,
             )
@@ -457,23 +538,33 @@
                 device_id_type=MESH,
             )
 
-        def backward(block, map_block, o_ref):
-            total = backward_body(block[0, 0], map_block[0, 0], xi_ref, yi_ref)
-            for j in range(1, per):
-                total += backward_body(block[j, 0], map_block[j, 0], xi_ref, yi_ref)
-            total = total.astype(o_ref.dtype)
+        def add(one, other):
+            return (one.astype(jnp.float32) + other.astype(jnp.float32)).astype(jnp.bfloat16)
+
+        def backward(block, map_block, early, o_ref):
+            total = backward_body(block[0], map_block[0], xi_ref, yi_ref)
             for i in range(pencils):
-                o_ref[i % 2, 0, i // 2] = total[i * rows : (i + 1) * rows]
-
-        plane = pl.BlockSpec((per, 1, lines, width), lambda c: (0, c, 0, 0))
+                block_sum = total[i * rows : (i + 1) * rows]
+                for j in range(last):
+                    block_sum += early[j, i % 2, 0, i // 2].astype(jnp.float32)
+                o_ref[i % 2, 0, i // 2] = block_sum.astype(o_ref.dtype)
+
+        plane = pl.BlockSpec((1, lines, width), lambda c: (c, 0, 0))
+        early_spec = pl.BlockSpec((last, 2, 1, chips, rows, width), lambda c: (0, 0, c, 0, 0, 0))
         part_spec = pl.BlockSpec((2, 1, chips, rows, width), lambda c: (0, c, 0, 0, 0))
 
         def step(t, carry):
             @pl.when(t < share)
             def _():
                 pltpu.emit_pipeline(
-                    backward, grid=(columns,), in_specs=[plane, plane], out_specs=[part_spec]
-                )(vol_ref.at[:, :, t], map_ref.at[:, :, t], part_ref.at[t])
+                    backward,
+                    grid=(columns,),
+                    in_specs=[plane, plane, early_spec],
+                    out_specs=[part_spec],
+                )(
+                    vol_ref.at[last, :, t], map_ref.at[last, :, t], early_ref.at[:, t],
+                    part_ref.at[t],
+                )
                 core_copy(t).start()
                 own_copy(t).start()
 
@@ -484,29 +575,34 @@
                 core_copy(k).wait_recv()
                 for c in range(columns):
                     for z in range(chips):
-                        mine[k, c, z] = (
-                            mine[k, c, z].astype(jnp.float32)
-                            + from_core[k, c, z].astype(jnp.float32)
-                        ).astype(jnp.bfloat16)
-                for s in range(1, columns):
-                    column_copy(k, s).start()
+                        mine[k, c, z] = add(mine[k, c, z], from_core[k, c, z])
+                for h in range(2):
+                    for n in range(2):
+                        one_copy(k, h, n).start()
 
             @pl.when((t >= 2) & (t < share + 2))
             def _():
                 k = t - 2
-                for s in range(1, columns):
-                    column_copy(k, s).wait_recv()
-                for z in range(chips):
-                    total = mine[k, column, z].astype(jnp.float32)
-                    for s in range(1, columns):
-                        total += from_column[k, s - 1, z].astype(jnp.float32)
-                    column_sum[k, z] = total.astype(jnp.bfloat16)
+                for h in range(2):
+                    other = flip(column, 2 - h)
+                    for n in range(2):
+                        one_copy(k, h, n).wait_recv()
+                    mine[k, other, side[h]] = add(mine[k, other, side[h]], from_first[k, h, 1])
+                    two_copy(k, h).start()
+                    mine[k, column, side[h]] = add(mine[k, column, side[h]], from_first[k, h, 0])
+
+            @pl.when((t >= 3) & (t < share + 3))
+            def _():
+                k = t - 3
+                for h in range(2):
+                    two_copy(k, h).wait_recv()
+                    column_sum[k, side[h]] = add(mine[k, column, side[h]], from_second[k, h])
                 for s in range(1, chips):
                     chip_copy(k, s).start()
 
-            @pl.when(t >= 3)
+            @pl.when(t >= 4)
             def _():
-                k = t - 3
+                k = t - 4
                 for s in range(1, chips):
                     chip_copy(k, s).wait_recv()
                 total = column_sum[k, chip].astype(jnp.float32)
@@ -516,12 +612,14 @@
 
             return carry
 
-        lax.fori_loop(0, share + 3, step, 0)
+        lax.fori_loop(0, share + 4, step, 0)
 
         def finish(k, carry):
             core_copy(k).wait_send()
-            for s in range(1, columns):
-                column_copy(k, s).wait_send()
+            for h in range(2):
+                for n in range(2):
+                    one_copy(k, h, n).wait_send()
+                two_copy(k, h).wait_send()
             for s in range(1, chips):
                 chip_copy(k, s).wait_send()
             return carry
@@ -538,19 +636,22 @@
             jax.ShapeDtypeStruct((share, 2, columns) + block, jnp.bfloat16),
             jax.ShapeDtypeStruct((share, rows, width), jnp.float32),
         ],
-        in_specs=[anywhere, anywhere, vmem, vmem],
+        in_specs=[anywhere, anywhere, anywhere, vmem, vmem],
         out_specs=[anywhere, vmem],
         scratch_shapes=[
             pltpu.VMEM((share, columns) + block, jnp.bfloat16),
             pltpu.VMEM((share, columns) + block, jnp.bfloat16),
-            pltpu.VMEM((share, columns - 1) + block, jnp.bfloat16),
+            pltpu.VMEM((share, 2, 2, chips // 2, rows, width), jnp.bfloat16),
+            pltpu.VMEM((share, 2, chips // 2, rows, width), jnp.bfloat16),
             pltpu.VMEM((share,) + block, jnp.bfloat16),
             pltpu.VMEM((share, chips - 1, rows, width), jnp.bfloat16),
             dma((share,)),
             dma((share,)),
             dma((share,)),
-            dma((share, columns - 1)),
-            dma((share, columns - 1)),
+            dma((share, 4)),
+            dma((share, 4)),
+            dma((share, 2)),
+            dma((share, 2)),
             dma((share, chips - 1)),
             dma((share, chips - 1)),
         ],
@@ -558,7 +659,7 @@
             collective_id=1, has_side_effects=True, vmem_limit_bytes=60 << 20
         ),
         name="backward_combine",
-    )(volume, maps, x_inv, y_inv)[1]
+    )(volume, maps, parts, x_inv, y_inv)[1]
 
 
 def plan_mask(sample_mask, readout):
@@ -574,19 +675,20 @@
     slices = object_image.shape[0]
     lines = object_image.shape[1] * lax.axis_size("pencil")
     group = 16
-    x_fwd, x_inv, y_fwd, y_inv, z_fwd, z_inv = plan_tables(slices, lines, readout, group)
+    tables = plan_tables(slices, lines, readout, group)
     mask = plan_mask(sample_mask, readout)
-    maps, _, _, volume = exchange_call(
-        coil_maps, object_image, mask, x_fwd, y_fwd, z_fwd, z_inv, group
-    )
-    return combine_call(volume, maps, x_inv, y_inv)
+    maps, _, _, volume, parts = exchange_call(coil_maps, object_image, mask, tables, group, 4)
+    return combine_call(volume, maps, parts, tables[1], tables[3])
 
 
 def solution(mesh):
     placed = (P(None, "pencil", None), P("coil", None, "pencil", None), P())
 
     def on_device(object_image, coil_maps, sample_mask):
-        whole = coil_maps.shape[0] % lax.axis_size("pencil") == 0
+        pencils = lax.axis_size("pencil")
+        whole = coil_maps.shape[0] % pencils == 0 and coil_maps.shape[0] >= 2 * pencils
+        whole = whole and pencils >= 4 and pencils & (pencils - 1) == 0
+        whole = whole and lax.axis_size("coil") == 4
         return (whole_coils if whole else split_lines)(object_image, coil_maps, sample_mask)
 
     return jax.shard_map(

time: 969 us -> 945 us (0.975)
  Pallas kernels: 956 us -> 932 us
    pallas_call x1, Pallas kernels: 186 us -> 121 us  [combine_call(): pl.pallas_call(kernel, out_shape=[jax.ShapeDtypeStruct((share, 2, columns...]
    pallas_call x1, Pallas kernels: 771 us -> 811 us  [exchange_call(): pl.pallas_call(kernel, out_shape=[whole, jax.ShapeDtypeStruct((2, slices,...]
where the time goes in v3:
time: 945 us; the launch traced here: 940 us
  Pallas kernels  932 us (99%)
    pallas_call x1, Pallas kernels, exchange_call(): pl.pallas_call(kernel, out_shape=[whole, jax.ShapeDtypeStruct((2, slices,...  811 us
    pallas_call x1, Pallas kernels, combine_call(): pl.pallas_call(kernel, out_shape=[jax.ShapeDtypeStruct((share, 2, columns...  121 us

profile of v3, /device:TPU:0, one launch (start us, length us, event | category | flops | bytes accessed | tf_op | source)
XLA Modules:
  0.0 940.3 jit_solution(9736997873556237071)
XLA Ops:
  0.0 0.9 compare_convert_fusion
  0.9 1.1 copy.10
  2.0 1.3 copy.14
  3.4 0.2 broadcast_in_dim.3
  3.6 2.4 copy.13.mask_ref
  5.9 810.9 %exchange_forward.1 = (bf16[2,32,256,1024]{3,2,1,0:T(8,128)(2,1)}, bf16[2,32,4,32,1024]{4,3,2,1,0:T(8,128)(2,1)}, bf16[2,32,256,1024]{3,2,1,0:T(8,128)(2,1)}, bf...) custom-call(bf16[16,32,32,1024]{3,2,1,0:T(8,128)(2,1)} %map_ref.1, bf16[32,32,1024]{2,1,0:T(8,128)(2,1)} %image_ref.1, ...), custom_call_target="tpu_custom_call" | custom-call | tf_op jit(solution)/shard_map/exchange_forward/pallas_call | solution.py:437
  816.8 121.2 %backward_combine.1 = (bf16[8,2,4,4,32,1024]{5,4,3,2,1,0:T(8,128)(2,1)}, f32[8,32,1024]{2,1,0:T(8,128)}) custom-call(bf16[2,4,8,256,1024]{4,3,2,1,0:T(8,128)(2,1)} %bitcast.9, bf16[2,4,8,256,1024]{4,3,2,1,0:T(8,128)(2,1)} %bitcast.8, bf16[1,8,2,4,4,32,1024]{6,5,4,3,2,1,0:T(8,128)(2,1)} %get-tuple-element.11.early_ref, ...), custom_call_target="tpu_custom_call" | custom-call | tf_op jit(solution)/shard_map/backward_combine/pallas_call | solution.py:633
  938.0 2.3 copy.17
  (1 shorter events, 0.0 us)
